TPU v7x, 512 devices: a whole 4x8x8 slice. The times are simulated.
512 devices in a mesh: seq: 128 (over z, y, core), head: 4 (over x).
Axes of the slice: x: 4, y: 8, z: 8, core: 2. Of those that a mesh axis runs over, the one named last changes fastest.
Arguments:
- queries: bfloat16 [65536, 4096], P('seq', 'head'), may hold values from -6 to 6
- keys: bfloat16 [65536, 4096], P('seq', 'head'), may hold values from -6 to 6
- values: bfloat16 [65536, 4096], P('seq', 'head'), may hold values from -6 to 6
- level_weights: float32 [9, 32, 65536], P(None, 'head', 'seq'), may hold values from 0.1 to 3, as said below
- norm_gain: float32 [4096], P('head'), may hold values from 0.25 to 1.75
Outputs:
- mixed: bfloat16 [65536, 4096], P('seq', 'head')
Inputs may be any that keep to these rules, and one draw needn't show every extreme that they name: `level_weights`: positive level weights.
All inputs are finite; a program needn't handle non-finite values.
Results may differ from a plain program's by a relative error of at most 0.0049.
Values may be sent and summed in bfloat16 or wider, within the bound.
A program may use at most 64 MiB of HBM per device.

v0:
```python
import jax
import jax.numpy as jnp
from jax import lax
from jax.sharding import PartitionSpec as P

HEAD_DIM = 128
STRETCH = 256
D = 4096


EPSILON = 1e-06


def swapped(block, axis, stride):
    count = lax.axis_size(axis)
    route = []
    for low in range(count):
        high = low | 1 << stride
        if high != low and high < count:
            route += [(low, high), (high, low)]
    return lax.ppermute(block, axis, route)


def shifted(block, axis, distance):
    devices = range(lax.axis_size(axis))
    route = [(i - distance, i) for i in devices if i - distance in devices]
    return lax.ppermute(block, axis, route)


def from_everyone(value, axis):
    copies = jnp.broadcast_to(value, (lax.axis_size(axis), *value.shape))
    return lax.all_to_all(copies, axis, split_axis=0, concat_axis=0, tiled=True)


def taken_together(value, axis):
    return from_everyone(value, axis).sum(axis=0)


def local(queries, keys, values, level_weights, norm_gain):
    tok_rows = queries.shape[0]
    heads_here = queries.shape[1] // HEAD_DIM
    stretch_count = tok_rows // STRETCH
    block_shape = (stretch_count, STRETCH, heads_here, HEAD_DIM)
    query_block_list = queries.reshape(block_shape)
    key_blocks = keys.reshape(block_shape)
    value_blocks = values.reshape(block_shape)
    level_total = level_weights.shape[0]
    weights_here = level_weights.reshape(level_total, heads_here, stretch_count, STRETCH).transpose(
        0, 2, 3, 1
    )
    states = jnp.einsum(
        "cthk,cthv->chkv", key_blocks, value_blocks, preferred_element_type=jnp.float32
    )
    scores = jnp.einsum(
        "cthk,cshk->chts", query_block_list, key_blocks, preferred_element_type=jnp.float32
    )
    causal = lax.broadcasted_iota(jnp.int32, (STRETCH, STRETCH), 0) >= lax.broadcasted_iota(
        jnp.int32, (STRETCH, STRETCH), 1
    )
    attn_probs = jnp.where(causal[None, None], scores, 0.0).astype(jnp.bfloat16)
    intra_out = jnp.einsum(
        "chts,cshv->cthv", attn_probs, value_blocks, preferred_element_type=jnp.float32
    )
    combined = weights_here[0][..., None] * intra_out
    running = states
    local_bits = stretch_count.bit_length() - 1
    level_bit = 0
    groups = running.shape[0] // 2
    block_span = 2**level_bit
    halves = running.reshape(groups, 2, heads_here, HEAD_DIM, HEAD_DIM)
    leftward_sum = halves[:, 0].astype(jnp.bfloat16)
    rightward_queries = query_block_list.reshape(
        groups, 2, block_span * STRETCH, heads_here, HEAD_DIM
    )[:, 1]
    state_readout = jnp.einsum(
        "nthk,nhkv->nthv", rightward_queries, leftward_sum, preferred_element_type=jnp.float32
    )
    level_weight = weights_here[1 + level_bit].reshape(groups, 2, block_span * STRETCH, heads_here)[
        :, 1
    ]
    contrib = level_weight[..., None] * state_readout
    padded = jnp.stack([jnp.zeros_like(contrib), contrib], axis=1)
    combined = combined + padded.reshape(stretch_count, STRETCH, heads_here, HEAD_DIM)
    running = halves[:, 0] + halves[:, 1]
    device_sum = running[0]
    seq_count = lax.axis_size("seq")
    seq_bits = seq_count.bit_length() - 1
    position = lax.axis_index("seq")
    crossing_state_list = []
    for level_bit in range(seq_bits - 1):
        partner = swapped(device_sum, "seq", level_bit)
        is_right = position >> level_bit & 1 == 1
        crossing_state_list.append(
            jnp.where(is_right, partner, jnp.zeros_like(partner)).astype(jnp.bfloat16)
        )
        device_sum = device_sum + partner
    last_partner = shifted(device_sum.astype(jnp.bfloat16), "seq", seq_count // 2)
    crossing_state_list.append(last_partner)
    for number, state_per_level in enumerate(crossing_state_list):
        state_readout = jnp.einsum(
            "lwnx,nxq->lwnq", query_block_list, state_per_level, preferred_element_type=jnp.float32
        )
        combined = combined + weights_here[1 + local_bits + number][..., None] * state_readout
    squares = jnp.sum(combined * combined, axis=(2, 3)).reshape(tok_rows)
    total_squares = taken_together(squares, "head")
    inverse_rms = lax.rsqrt(total_squares / D + EPSILON)
    flat_out = combined.reshape(tok_rows, heads_here * HEAD_DIM)
    mixed_out = flat_out * inverse_rms[:, None] * norm_gain[None, :]
    return mixed_out.astype(jnp.bfloat16)


def solution(mesh):
    return jax.shard_map(
        local,
        mesh=mesh,
        in_specs=(
            P("seq", "head"),
            P("seq", "head"),
            P("seq", "head"),
            P(None, "head", "seq"),
            P("head"),
        ),
        out_specs=P("seq", "head"),
        check_vma=False,
    )
```

profile of v0, /device:TPU:120, one launch (start us, length us, event | category | flops | bytes accessed | tf_op | source)
XLA Modules:
  0.0 165.2 jit_solution(1085753345159035951)
XLA Ops:
  0.0 1.6 copy.121
  1.6 0.7 copy.83
  2.6 1.0 copy-done
  4.0 1.9 %collective-permute-start = (f32[8,128,128]{2,1,0:T(8,128)S(1)}, f32[8,128,128]{2,1,0:T(8,128)S(1)}, u32[]{:S(2)}, u32[]{:S(2)}) collective-permute-start(f32[8,128,128]{2,1,0:T(8,128)S(1)} %fusion.14), channel_id=1, source_target_pairs={{0,4},{4,0},{8,12},{12,8},{16,20},{20,16},{24,28},{28,24},{32,36},... | collective-permute-start | bytes 1572872 | tf_op jit(solution)/shard_map/ppermute | solution.py:21
  6.0 1.9 %collective-permute-done = f32[8,128,128]{2,1,0:T(8,128)S(1)} collective-permute-done((f32[8,128,128]{2,1,0:T(8,128)S(1)}, f32[8,128,128]{2,1,0:T(8,128)S(1)}, u32[]{:S(2)}, u32[]{:S(2)}) %collective-permute-start) | collective-permute-done | bytes 524320 | tf_op jit(solution)/shard_map/ppermute | solution.py:21
  7.8 0.8 copy-done.3
  8.6 0.9 fusion.66
  9.5 3.4 %collective-permute-start.1 = (f32[8,128,128]{2,1,0:T(8,128)}, f32[8,128,128]{2,1,0:T(8,128)}, u32[]{:S(2)}, u32[]{:S(2)}) collective-permute-start(f32[8,128,128]{2,1,0:T(8,128)} %fusion.66), channel_id=1, source_target_pairs={{0,8},{8,0},{4,12},{12,4},{16,24},{24,16},{20,28},{28,20},{32,40},... | collective-permute-start | bytes 1572872 | tf_op jit(solution)/shard_map/ppermute | solution.py:21
  12.9 1.5 copy.120
  14.5 11.3 %collective-permute-done.1 = f32[8,128,128]{2,1,0:T(8,128)} collective-permute-done((f32[8,128,128]{2,1,0:T(8,128)}, f32[8,128,128]{2,1,0:T(8,128)}, u32[]{:S(2)}, u32[]{:S(2)}) %collective-permute-start.1) | collective-permute-done | bytes 524320 | tf_op jit(solution)/shard_map/ppermute | solution.py:21
  25.8 2.0 %add.69 = f32[8,128,128]{2,1,0:T(8,128)} add(f32[8,128,128]{2,1,0:T(8,128)} %fusion.66, f32[8,128,128]{2,1,0:T(8,128)} %collective-permute-done.1) | non-fusion elementwise | flops 131072 | bytes 1572864 | tf_op jit(solution)/shard_map/add | solution.py:96
  27.8 4.0 %collective-permute-start.2 = (f32[8,128,128]{2,1,0:T(8,128)}, f32[8,128,128]{2,1,0:T(8,128)}, u32[]{:S(2)}, u32[]{:S(2)}) collective-permute-start(f32[8,128,128]{2,1,0:T(8,128)} %add.69), channel_id=1, source_target_pairs={{0,16},{16,0},{4,20},{20,4},{8,24},{24,8},{12,28},{28,12},{32,48},... | collective-permute-start | bytes 1572872 | tf_op jit(solution)/shard_map/ppermute | solution.py:21
  31.9 1.3 fusion.11
  33.2 3.9 %fusion.9 = f32[2,8,256,128]{2,3,1,0:T(8,128)} fusion(bf16[2,256,8,128]{1,3,2,0:T(8,128)(2,1)S(1)} %copy.83, pred[256,256]{1,0:T(8,128)(4,1)S(1)} %iota_compare_fusion, bf16[2,256,8,128]{3,2,1,0:T(8,128)(2,1)} %bitcast.149, bf16[2,256,8,128]{3,2,1,0:T(8,128)(2,1)S(1)} %bitcast.139), kind=kOutput, calls=%fused_computation.21 | convolution fusion | flops 538968064 | bytes 5308416 | tf_op jit(solution)/shard_map/chts,cshv->cthv/dot_general | solution.py:61
  37.1 18.2 %collective-permute-done.2 = f32[8,128,128]{2,1,0:T(8,128)} collective-permute-done((f32[8,128,128]{2,1,0:T(8,128)}, f32[8,128,128]{2,1,0:T(8,128)}, u32[]{:S(2)}, u32[]{:S(2)}) %collective-permute-start.2) | collective-permute-done | bytes 524320 | tf_op jit(solution)/shard_map/ppermute | solution.py:21
  55.3 1.3 add.71
  56.6 4.6 %collective-permute-start.3 = (f32[8,128,128]{2,1,0:T(8,128)S(1)}, f32[8,128,128]{2,1,0:T(8,128)S(1)}, u32[]{:S(2)}, u32[]{:S(2)}) collective-permute-start(f32[8,128,128]{2,1,0:T(8,128)S(1)} %add.71), channel_id=1, source_target_pairs={{0,32},{32,0},{4,36},{36,4},{8,40},{40,8},{12,44},{44,12},{16,48},... | collective-permute-start | bytes 1572872 | tf_op jit(solution)/shard_map/ppermute | solution.py:21
  61.7 24.9 %collective-permute-done.3 = f32[8,128,128]{2,1,0:T(8,128)S(1)} collective-permute-done((f32[8,128,128]{2,1,0:T(8,128)S(1)}, f32[8,128,128]{2,1,0:T(8,128)S(1)}, u32[]{:S(2)}, u32[]{:S(2)}) %collective-permute-start.3) | collective-permute-done | bytes 524320 | tf_op jit(solution)/shard_map/ppermute | solution.py:21
  86.7 1.9 %collective-permute-start.4 = (f32[8,128,128]{2,1,0:T(8,128)S(1)}, f32[8,128,128]{2,1,0:T(8,128)S(1)}, u32[]{:S(2)}, u32[]{:S(2)}) collective-permute-start(f32[8,128,128]{2,1,0:T(8,128)S(1)} %add.73), channel_id=1, source_target_pairs={{0,64},{64,0},{4,68},{68,4},{8,72},{72,8},{12,76},{76,12},{16,80},... | collective-permute-start | bytes 1572872 | tf_op jit(solution)/shard_map/ppermute | solution.py:21
  88.6 1.6 fusion.21
  90.2 1.6 fusion.24
  91.7 10.5 %collective-permute-done.4 = f32[8,128,128]{2,1,0:T(8,128)S(1)} collective-permute-done((f32[8,128,128]{2,1,0:T(8,128)S(1)}, f32[8,128,128]{2,1,0:T(8,128)S(1)}, u32[]{:S(2)}, u32[]{:S(2)}) %collective-permute-start.4) | collective-permute-done | bytes 524320 | tf_op jit(solution)/shard_map/ppermute | solution.py:21
  102.3 6.1 %collective-permute-start.5 = (f32[8,128,128]{2,1,0:T(8,128)S(1)}, f32[8,128,128]{2,1,0:T(8,128)S(1)}, u32[]{:S(2)}, u32[]{:S(2)}) collective-permute-start(f32[8,128,128]{2,1,0:T(8,128)S(1)} %add.75), channel_id=1, source_target_pairs={{0,128},{128,0},{4,132},{132,4},{8,136},{136,8},{12,140},{140,12},... | collective-permute-start | bytes 1572872 | tf_op jit(solution)/shard_map/ppermute | solution.py:21
  109.4 20.5 %collective-permute-done.5 = f32[8,128,128]{2,1,0:T(8,128)S(1)} collective-permute-done((f32[8,128,128]{2,1,0:T(8,128)S(1)}, f32[8,128,128]{2,1,0:T(8,128)S(1)}, u32[]{:S(2)}, u32[]{:S(2)}) %collective-permute-start.5) | collective-permute-done | bytes 524320 | tf_op jit(solution)/shard_map/ppermute | solution.py:21
  130.0 8.5 %collective-permute-start.6 = (bf16[8,128,128]{2,1,0:T(8,128)(2,1)S(1)}, bf16[8,128,128]{2,1,0:T(8,128)(2,1)S(1)}, u32[]{:S(2)}, u32[]{:S(2)}) collective-permute-start(bf16[8,128,128]{2,1,0:T(8,128)(2,1)S(1)} %add_convert_fusion), channel_id=1, source_target_pairs={{0,256},{4,260},{8,264},{12,268},{16,272},{20,276},{24,280},{28,28... | collective-permute-start | bytes 786440 | tf_op jit(solution)/shard_map/ppermute | solution.py:27
  139.0 10.8 %collective-permute-done.6 = bf16[8,128,128]{2,1,0:T(8,128)(2,1)S(1)} collective-permute-done((bf16[8,128,128]{2,1,0:T(8,128)(2,1)S(1)}, bf16[8,128,128]{2,1,0:T(8,128)(2,1)S(1)}, u32[]{:S(2)}, u32[]{:S(2)}) %collective-permute-start.6) | collective-permute-done | bytes 262176 | tf_op jit(solution)/shard_map/ppermute | solution.py:27
  149.8 2.1 %multiply_reduce_fusion = (f32[2,256]{1,0:T(2,128)S(1)}, f32[2,256,8,128]{1,3,2,0:T(8,128)S(1)}) fusion(bf16[2,256,8,128]{3,2,1,0:T(8,128)(2,1)S(1)} %bitcast.146, bf16[8,128,128]{2,1,0:T(8,128)(2,1)S(1)} %collective-permute-done.6, f32[2,256,8]{1,2,0:T(8,128)S(1)} %get-tuple-element.6, f32[8,128,2,256]{3,1,0,2:T(8,128)S(1)} %fusion.33, ...), kind=kOutput, calls=%fused_computation.20 | convolution fusion | flops 143654400 | bytes 19269632 | tf_op jit(solution)/shard_map/lwnx,nxq->lwnq/dot_general | solution.py:100
  152.0 0.6 broadcast_in_dim.23
  152.6 4.2 %all-to-all-start = ((f32[4,1,512]{2,1,0:T(1,128)}), f32[4,1,512]{2,1,0:T(1,128)S(1)}, u32[]{:S(2)}, u32[]{:S(2)}) async-start(f32[4,1,512]{2,1,0:T(1,128)} %broadcast_in_dim.23), calls=%async_computation | async-start | bytes 16384 | tf_op jit(solution)/shard_map/all_to_all | solution.py:32
  156.8 1.8 %copy.101 = f32[2,256,8,128]{3,2,1,0:T(8,128)} copy(f32[2,256,8,128]{1,3,2,0:T(8,128)S(1)} %get-tuple-element.14) | data formatting | bytes 4194304 | tf_op jit(solution)/shard_map/add | solution.py:103
  158.7 3.5 %all-to-all-done = f32[4,1,512]{2,1,0:T(1,128)S(1)} async-done(((f32[4,1,512]{2,1,0:T(1,128)}), f32[4,1,512]{2,1,0:T(1,128)S(1)}, u32[]{:S(2)}, u32[]{:S(2)}) %all-to-all-start) | async-done | bytes 8224 | tf_op jit(solution)/shard_map/all_to_all | solution.py:32
  162.2 3.0 %fusion.1 = bf16[512,1024]{1,0:T(8,128)(2,1)} fusion(f32[64,8,8,128]{3,2,1,0:T(8,128)} %bitcast.147, f32[1024]{0:T(1024)S(1)} %copy-done.7, f32[512]{0:T(512)S(1)} %add_rsqrt_fusion), kind=kLoop, calls=%fused_computation.3 | loop fusion | flops 1572864 | bytes 3151872 | tf_op jit(solution)/shard_map/convert_element_type | solution.py:109
  (31 shorter events, 3.1 us)
Async XLA Ops:
  0.0 2.3 %copy-start.5 = (bf16[512,1024]{1,0:T(8,128)(2,1)S(1)}, bf16[512,1024]{1,0:T(8,128)(2,1)}, u32[]{:S(2)}) copy-start(bf16[512,1024]{1,0:T(8,128)(2,1)} %param.7) | copy-start | bytes 3145732
  2.6 1.0 copy-start
  4.0 3.8 %collective-permute-start = (f32[8,128,128]{2,1,0:T(8,128)S(1)}, f32[8,128,128]{2,1,0:T(8,128)S(1)}, u32[]{:S(2)}, u32[]{:S(2)}) collective-permute-start(f32[8,128,128]{2,1,0:T(8,128)S(1)} %fusion.14), channel_id=1, source_target_pairs={{0,4},{4,0},{8,12},{12,8},{16,20},{20,16},{24,28},{28,24},{32,36},... | collective-permute-start | bytes 1572872 | tf_op jit(solution)/shard_map/ppermute | solution.py:21
  7.8 0.8 copy-start.3
  9.5 5.0 %copy-start.6 = (f32[9,8,512]{2,1,0:T(8,128)S(1)}, f32[9,8,512]{2,1,0:T(8,128)}, u32[]{:S(2)}) copy-start(f32[9,8,512]{2,1,0:T(8,128)} %param.8) | copy-start | bytes 442372
  9.5 16.3 %collective-permute-start.1 = (f32[8,128,128]{2,1,0:T(8,128)}, f32[8,128,128]{2,1,0:T(8,128)}, u32[]{:S(2)}, u32[]{:S(2)}) collective-permute-start(f32[8,128,128]{2,1,0:T(8,128)} %fusion.66), channel_id=1, source_target_pairs={{0,8},{8,0},{4,12},{12,4},{16,24},{24,16},{20,28},{28,20},{32,40},... | collective-permute-start | bytes 1572872 | tf_op jit(solution)/shard_map/ppermute | solution.py:21
  27.8 27.5 %collective-permute-start.2 = (f32[8,128,128]{2,1,0:T(8,128)}, f32[8,128,128]{2,1,0:T(8,128)}, u32[]{:S(2)}, u32[]{:S(2)}) collective-permute-start(f32[8,128,128]{2,1,0:T(8,128)} %add.69), channel_id=1, source_target_pairs={{0,16},{16,0},{4,20},{20,4},{8,24},{24,8},{12,28},{28,12},{32,48},... | collective-permute-start | bytes 1572872 | tf_op jit(solution)/shard_map/ppermute | solution.py:21
  37.1 24.1 %copy-start.4 = (f32[8,128,128]{2,1,0:T(8,128)S(1)}, f32[8,128,128]{2,1,0:T(8,128)}, u32[]{:S(2)}) copy-start(f32[8,128,128]{2,1,0:T(8,128)} %copy-done.3) | copy-start | bytes 1572868
  56.6 30.0 %collective-permute-start.3 = (f32[8,128,128]{2,1,0:T(8,128)S(1)}, f32[8,128,128]{2,1,0:T(8,128)S(1)}, u32[]{:S(2)}, u32[]{:S(2)}) collective-permute-start(f32[8,128,128]{2,1,0:T(8,128)S(1)} %add.71), channel_id=1, source_target_pairs={{0,32},{32,0},{4,36},{36,4},{8,40},{40,8},{12,44},{44,12},{16,48},... | collective-permute-start | bytes 1572872 | tf_op jit(solution)/shard_map/ppermute | solution.py:21
  86.7 15.6 %collective-permute-start.4 = (f32[8,128,128]{2,1,0:T(8,128)S(1)}, f32[8,128,128]{2,1,0:T(8,128)S(1)}, u32[]{:S(2)}, u32[]{:S(2)}) collective-permute-start(f32[8,128,128]{2,1,0:T(8,128)S(1)} %add.73), channel_id=1, source_target_pairs={{0,64},{64,0},{4,68},{68,4},{8,72},{72,8},{12,76},{76,12},{16,80},... | collective-permute-start | bytes 1572872 | tf_op jit(solution)/shard_map/ppermute | solution.py:21
  102.3 27.6 %collective-permute-start.5 = (f32[8,128,128]{2,1,0:T(8,128)S(1)}, f32[8,128,128]{2,1,0:T(8,128)S(1)}, u32[]{:S(2)}, u32[]{:S(2)}) collective-permute-start(f32[8,128,128]{2,1,0:T(8,128)S(1)} %add.75), channel_id=1, source_target_pairs={{0,128},{128,0},{4,132},{132,4},{8,136},{136,8},{12,140},{140,12},... | collective-permute-start | bytes 1572872 | tf_op jit(solution)/shard_map/ppermute | solution.py:21
  130.0 19.8 %copy-start.1 = (f32[1,1,256,8,128]{2,4,3,1,0:T(8,128)S(1)}, f32[1,1,256,8,128]{2,4,3,1,0:T(8,128)}, u32[]{:S(2)}) copy-start(f32[1,1,256,8,128]{2,4,3,1,0:T(8,128)} %fusion.11) | copy-start | bytes 3145732
  130.0 19.8 %copy-start.2 = (f32[2,8,256,128]{2,3,1,0:T(8,128)S(1)}, f32[2,8,256,128]{2,3,1,0:T(8,128)}, u32[]{:S(2)}) copy-start(f32[2,8,256,128]{2,3,1,0:T(8,128)} %fusion.9) | copy-start | bytes 6291460
  130.0 19.8 %collective-permute-start.6 = (bf16[8,128,128]{2,1,0:T(8,128)(2,1)S(1)}, bf16[8,128,128]{2,1,0:T(8,128)(2,1)S(1)}, u32[]{:S(2)}, u32[]{:S(2)}) collective-permute-start(bf16[8,128,128]{2,1,0:T(8,128)(2,1)S(1)} %add_convert_fusion), channel_id=1, source_target_pairs={{0,256},{4,260},{8,264},{12,268},{16,272},{20,276},{24,280},{28,28... | collective-permute-start | bytes 786440 | tf_op jit(solution)/shard_map/ppermute | solution.py:27
  152.6 9.6 %all-to-all-start = ((f32[4,1,512]{2,1,0:T(1,128)}), f32[4,1,512]{2,1,0:T(1,128)S(1)}, u32[]{:S(2)}, u32[]{:S(2)}) async-start(f32[4,1,512]{2,1,0:T(1,128)} %broadcast_in_dim.23), calls=%async_computation | async-start | bytes 16384 | tf_op jit(solution)/shard_map/all_to_all | solution.py:32
  156.8 5.4 %copy-start.7 = (f32[1024]{0:T(1024)S(1)}, f32[1024]{0:T(1024)}, u32[]{:S(2)}) copy-start(f32[1024]{0:T(1024)} %param.9) | copy-start | bytes 12292
where the time goes:
time: 166 us; the launch traced here: 165 us
  waiting for transfers between devices  102 us (61%)
  starting transfers between devices  34.7 us (21%)
  matrix products  12.8 us (8%)
  local copies, waits for them, and re-layouts  8.3 us (5%)
  other arithmetic  7.44 us (4%)
    ppermute x6, waiting for transfers between devices, swapped(): return lax.ppermute(block, axis, route)  87.3 us
    ppermute x6, starting transfers between devices, swapped(): return lax.ppermute(block, axis, route)  21.9 us
    ppermute x1, waiting for transfers between devices, shifted(): return lax.ppermute(block, axis, route)  10.8 us
    ppermute x1, starting transfers between devices, shifted(): return lax.ppermute(block, axis, route)  8.48 us
    dot_general x7, matrix products, local(): jnp.einsum('lwnx,nxq->lwnq', query_block_list, state_per_level, preferred...  7.23 us
    unnamed x20, local copies, waits for them, and re-layouts  5.12 us
    add x5, other arithmetic, local(): device_sum = device_sum + partner  4.29 us
    all_to_all x1, starting transfers between devices, from_everyone(): return lax.all_to_all(copies, axis, split_axis=0, concat_axis=0, tiled=True)  4.25 us
  transfers between devices with their start and end apart: 8, of which 8 were waited for; matrix products, arithmetic and copies ran while one was open for 8% of the time, Pallas kernels for 0%

commit v1 on v0

v1 whole, which is shorter than its diff:
```python
import jax
import jax.numpy as jnp
from jax import lax
from jax.experimental import pallas as pl
from jax.experimental.pallas import tpu as pltpu
from jax.sharding import PartitionSpec as P

HEAD_DIM = 128
STRETCH = 256
D = 4096
EPSILON = 1e-06

RING = 8
COLS = 4
HEADS_HERE = 8
TOK = 512
HALF = 64
FAR_FIRST = (4, 3, 5, 2, 6, 1, 7)
NEAR_FIRST = (1, 7, 2, 6, 3, 5, 4)
MESH = pl.DeviceIdType.MESH
F32 = jnp.float32
BF16 = jnp.bfloat16


def nt(a, b):
    return lax.dot_general(a, b, (((1,), (1,)), ((), ())), preferred_element_type=F32)


def tn(a, b):
    return lax.dot_general(a, b, (((0,), (0,)), ((), ())), preferred_element_type=F32)


def nn(a, b):
    return jnp.dot(a, b, preferred_element_type=F32)


def kernel(
    q_hbm, k_hbm, v_hbm, w_hbm, g_hbm, out_hbm,
    q_s, k_s, v_s, w_v, g_v, w_rows, w_cols, out_s,
    first, own_sum, own_bf, pair_in, core0, chip_sum, ring_in, ring_sum, totals, low, high,
    acc, sq, sq_in,
    load_sem, misc_sem, out_sem,
    pair_send, pair_recv, core_send, core_recv, ring_send, ring_recv, next_send, next_recv,
    low_send, low_recv, tot_send, tot_recv, high_send, high_recv,
    fwl_send, fwl_recv, fwh_send, fwh_recv, sq_send, sq_recv,
):
    seq = lax.axis_index("seq")
    col = lax.axis_index("head")
    core = lax.rem(seq, 2)
    y = lax.rem(seq // 2, RING)
    z = seq // (2 * RING)

    def device(z_, y_, core_):
        return (z_ * (2 * RING) + y_ * 2 + core_, col)

    sibling = device(z, y, 1 - core)
    mine = pl.ds(pl.multiple_of(core * HALF, HALF), HALF)
    other = pl.ds(pl.multiple_of((1 - core) * HALF, HALF), HALF)

    def row_peer(d):
        return lax.rem(y + d, RING)

    def col_peer(d):
        return lax.rem(z + d, RING)

    def remote(src, dst, send, recv, target):
        return pltpu.make_async_remote_copy(
            src_ref=src, dst_ref=dst, send_sem=send, recv_sem=recv, device_id=target, device_id_type=MESH
        )

    loads = {}
    for name, src, dst, slot in (("k", k_hbm, k_s, 0), ("v", v_hbm, v_s, 1), ("q", q_hbm, q_s, 2)):
        for h in range(HEADS_HERE):
            loads[name, h] = pltpu.make_async_copy(
                src.at[:, pl.ds(h * HEAD_DIM, HEAD_DIM)], dst.at[h], load_sem.at[slot, h]
            )
    for h in range(HEADS_HERE):
        loads["k", h].start()
        loads["v", h].start()
    w_load = pltpu.make_async_copy(w_hbm, w_v, misc_sem.at[0])
    g_load = pltpu.make_async_copy(g_hbm, g_v, misc_sem.at[1])

    barrier = pltpu.get_barrier_semaphore()
    pl.semaphore_signal(barrier, inc=1, device_id=sibling, device_id_type=MESH)
    for d in range(1, RING):
        pl.semaphore_signal(barrier, inc=1, device_id=device(z, row_peer(d), core), device_id_type=MESH)
        pl.semaphore_signal(barrier, inc=1, device_id=device(col_peer(d), y, core), device_id_type=MESH)
    for d in range(1, COLS):
        pl.semaphore_signal(barrier, inc=1, device_id=(seq, lax.rem(col + d, COLS)), device_id_type=MESH)

    for h in range(HEADS_HERE):
        loads["q", h].start()
    w_load.start()
    g_load.start()
    for h in range(HEADS_HERE):
        loads["k", h].wait()
        loads["v", h].wait()

    order = FAR_FIRST + (0,)

    def to_sibling(i, h):
        return remote(own_sum.at[h, other, :], pair_in.at[h], pair_send.at[i], pair_recv.at[i], sibling)

    for i, d in enumerate(order):
        h = row_peer(d)
        k = k_s[h]
        v = v_s[h]
        s0 = tn(k[:STRETCH], v[:STRETCH])
        s1 = tn(k[STRETCH:], v[STRETCH:])
        first[h] = s0.astype(BF16)
        s = s0 + s1
        own_sum[h] = s
        own_bf[h] = s.astype(BF16)
        if i == 0:
            pl.semaphore_wait(barrier, 1 + 2 * (RING - 1) + COLS - 1)
        to_sibling(i, h).start()

    to_core1 = remote(own_bf, core0, core_send, core_recv, sibling)

    @pl.when(core == 0)
    def _():
        to_core1.start()

    def to_owner(d):
        h = row_peer(d)
        return remote(chip_sum.at[h], ring_in.at[y], ring_send.at[d - 1], ring_recv.at[d - 1], device(z, h, core))

    for i, d in enumerate(order):
        h = row_peer(d)
        to_sibling(i, h).wait_recv()
        c = (own_sum[h, mine, :] + pair_in[h]).astype(BF16)
        chip_sum[h] = c
        if d:
            to_owner(d).start()
        else:
            ring_in[y] = c

    to_next = remote(
        chip_sum, low.at[0, :, mine, :], next_send, next_recv, device(z, lax.rem(y + 1, RING), core)
    )
    y0 = lax.rem(y, 2) == 1
    y1 = lax.rem(y // 2, 2) == 1
    y2 = y // 4 == 1

    @pl.when(jnp.logical_not(y0))
    def _():
        to_next.start()

    w_load.wait()
    for h in range(HEADS_HERE):
        for level in range(9):
            w_rows[h, level : level + 1, :] = w_v[level, h : h + 1, :]
        w_rows[h, 9:16, :] = jnp.zeros((7, TOK), F32)
    for h in range(HEADS_HERE):
        w_cols[h] = w_rows[h].T

    for h in range(HEADS_HERE):
        loads["q", h].wait()

    causal = lax.broadcasted_iota(jnp.int32, (STRETCH, STRETCH), 0) >= lax.broadcasted_iota(
        jnp.int32, (STRETCH, STRETCH), 1
    )

    def within(h):
        for s in range(2):
            rows = slice(s * STRETCH, (s + 1) * STRETCH)
            qs = q_s[h, rows, :]
            probs = jnp.where(causal, nt(qs, k_s[h, rows, :]), 0.0).astype(BF16)
            part = w_cols[h, rows, 0:1] * nn(probs, v_s[h, rows, :])
            if s == 1:
                part += w_cols[h, rows, 1:2] * nn(qs, first[h])
            acc[h, rows, :] = part

    for h in range(0, 5):
        within(h)

    for d in range(1, RING):
        to_owner(d).wait_recv()
    part = [ring_in[j].astype(F32) for j in range(RING)]
    s01 = part[0] + part[1]
    s0123 = s01 + (part[2] + part[3])
    s45 = part[4] + part[5]
    total = s0123 + (s45 + (part[6] + part[7]))
    totals[z] = total.astype(BF16)

    def to_column(d):
        return remote(
            totals.at[z], totals.at[z], tot_send.at[d - 1], tot_recv.at[d - 1], device(col_peer(d), y, core)
        )

    for d in FAR_FIRST:
        to_column(d).start()

    ring_sum[0] = s01.astype(BF16)
    ring_sum[1] = s45.astype(BF16)
    ring_sum[2] = s0123.astype(BF16)

    def low_copy(level, d):
        target = row_peer(d)
        src = ring_sum.at[target // 4] if level == 1 else ring_sum.at[2]
        return remote(
            src, low.at[level, y, mine, :], low_send.at[level - 1, d - 1], low_recv.at[level - 1, d - 1],
            device(z, target, core),
        )

    for d in FAR_FIRST:
        target = row_peer(d)

        @pl.when(lax.rem(target // 2, 2) == 1)
        def _():
            low_copy(1, d).start()

        @pl.when(target // 4 == 1)
        def _():
            low_copy(2, d).start()

    @pl.when(y1)
    def _():
        low[1, y, mine, :] = ring_sum[y // 4]

    @pl.when(y2)
    def _():
        low[2, y, mine, :] = ring_sum[2]

    for h in range(5, HEADS_HERE):
        within(h)

    for d in range(1, RING):
        to_column(d).wait_recv()
    zero = jnp.zeros((HALF, HEAD_DIM), F32)
    tot = lambda i: totals[i].astype(F32)
    z_even = z // 2 * 2
    z_four = z // 4 * 4
    odd = lax.rem(z, 2) == 1
    high[y, mine, 0:128] = jnp.where(odd, tot(z_even), zero).astype(BF16)
    high[y, mine, 128:256] = jnp.where(
        lax.rem(z // 2, 2) == 1, tot(z_four) + tot(z_four + 1), zero
    ).astype(BF16)
    high[y, mine, 256:384] = jnp.where(
        z // 4 == 1, (tot(0) + tot(1)) + (tot(2) + tot(3)), zero
    ).astype(BF16)

    def along_row(d):
        return remote(
            high.at[y, mine, :], high.at[y, mine, :], high_send.at[d - 1], high_recv.at[d - 1],
            device(z, row_peer(d), core),
        )

    for d in FAR_FIRST:
        along_row(d).start()

    def share_high(i, h):
        return remote(high.at[h, mine, :], high.at[h, mine, :], fwh_send.at[i], fwh_recv.at[i], sibling)

    share_high(0, y).start()

    @pl.when(core == 1)
    def _():
        to_core1.wait_recv()
        for h in range(HEADS_HERE):
            acc[h] += w_cols[h, :, 2:3] * nn(q_s[h], core0[h])

    def share_low(level):
        return remote(
            low.at[level, :, mine, :], low.at[level, :, mine, :], fwl_send.at[level], fwl_recv.at[level], sibling
        )

    conds = (y0, y1, y2)

    @pl.when(y0)
    def _():
        to_next.wait_recv()
        share_low(0).start()

    for level in (1, 2):

        @pl.when(conds[level])
        def _():
            for d in range(1, RING):
                low_copy(level, d).wait_recv()
            share_low(level).start()

    for level in range(3):

        @pl.when(conds[level])
        def _():
            share_low(level).wait_recv()
            for h in range(HEADS_HERE):
                acc[h] += w_cols[h, :, 3 + level : 4 + level] * nn(q_s[h], low[level, h])

    sq[...] = jnp.zeros_like(sq)

    def read_high(i, d):
        h = lax.rem(y + RING - d, RING)
        share_high(i, h).wait_recv()
        r = nn(q_s[h], high[h])
        a = acc[h]
        for level in range(3):
            a += w_cols[h, :, 6 + level : 7 + level] * r[:, level * 128 : (level + 1) * 128]
        acc[h] = a
        sq[...] += a * a

    arrivals = (0,) + NEAR_FIRST
    for i, d in enumerate(arrivals):
        if d:
            along_row(d).wait_recv()
            share_high(i, lax.rem(y + RING - d, RING)).start()
            read_high(i - 1, arrivals[i - 1])
    read_high(RING - 1, arrivals[RING - 1])

    sq_in[col, 0:1, :] = jnp.sum(sq[...].T, axis=0, keepdims=True)

    def to_cols(d):
        return remote(
            sq_in.at[col, 0:1], sq_in.at[col, 0:1], sq_send.at[d - 1], sq_recv.at[d - 1],
            (seq, lax.rem(col + d, COLS)),
        )

    for d in (2, 1, 3):
        to_cols(d).start()
    g_load.wait()
    for d in (1, 3, 2):
        to_cols(d).wait_recv()
    squares = (sq_in[0, 0:1, :] + sq_in[1, 0:1, :]) + (sq_in[2, 0:1, :] + sq_in[3, 0:1, :])
    inverse = lax.rsqrt(squares / D + EPSILON)
    scale = jnp.broadcast_to(inverse, (HEAD_DIM, TOK)).T

    def store(h):
        columns = pl.ds(h * HEAD_DIM, HEAD_DIM)
        return pltpu.make_async_copy(out_s.at[h], out_hbm.at[:, columns], out_sem.at[h])

    for h in range(HEADS_HERE):
        out_s[h] = (acc[h] * scale * g_v[:, h * HEAD_DIM : (h + 1) * HEAD_DIM]).astype(BF16)
        store(h).start()

    for i, d in enumerate(order):
        to_sibling(i, row_peer(d)).wait_send()

    @pl.when(core == 0)
    def _():
        to_core1.wait_send()

    @pl.when(jnp.logical_not(y0))
    def _():
        to_next.wait_send()

    for d in range(1, RING):
        to_owner(d).wait_send()
        to_column(d).wait_send()
        along_row(d).wait_send()
        target = row_peer(d)

        @pl.when(lax.rem(target // 2, 2) == 1)
        def _():
            low_copy(1, d).wait_send()

        @pl.when(target // 4 == 1)
        def _():
            low_copy(2, d).wait_send()

    for level in range(3):

        @pl.when(conds[level])
        def _():
            share_low(level).wait_send()

    for i, d in enumerate(arrivals):
        share_high(i, lax.rem(y + RING - d, RING)).wait_send()
    for d in range(1, COLS):
        to_cols(d).wait_send()
    for h in range(HEADS_HERE):
        store(h).wait()


def local(queries, keys, values, level_weights, norm_gain):
    hd, tok, half, ring = HEAD_DIM, TOK, HALF, RING
    dma = pltpu.SemaphoreType.DMA
    any_space = pl.BlockSpec(memory_space=pl.ANY)
    scratch = [
        pltpu.VMEM((8, tok, hd), BF16),
        pltpu.VMEM((8, tok, hd), BF16),
        pltpu.VMEM((8, tok, hd), BF16),
        pltpu.VMEM((9, 8, tok), F32),
        pltpu.VMEM((1, 1024), F32),
        pltpu.VMEM((8, 16, tok), F32),
        pltpu.VMEM((8, tok, 16), F32),
        pltpu.VMEM((8, tok, hd), BF16),
        pltpu.VMEM((8, hd, hd), BF16),
        pltpu.VMEM((8, hd, hd), F32),
        pltpu.VMEM((8, hd, hd), BF16),
        pltpu.VMEM((8, half, hd), F32),
        pltpu.VMEM((8, hd, hd), BF16),
        pltpu.VMEM((8, half, hd), BF16),
        pltpu.VMEM((ring, half, hd), BF16),
        pltpu.VMEM((3, half, hd), BF16),
        pltpu.VMEM((ring, half, hd), BF16),
        pltpu.VMEM((3, 8, hd, hd), BF16),
        pltpu.VMEM((8, hd, 3 * hd), BF16),
        pltpu.VMEM((8, tok, hd), F32),
        pltpu.VMEM((tok, hd), F32),
        pltpu.VMEM((COLS, 8, tok), F32),
        dma((3, 8)), dma((2,)), dma((8,)),
        dma((8,)), dma((8,)), dma, dma, dma((7,)), dma((7,)), dma, dma,
        dma((2, 7)), dma((2, 7)), dma((7,)), dma((7,)), dma((7,)), dma((7,)),
        dma((3,)), dma((3,)), dma((8,)), dma((8,)), dma((3,)), dma((3,)),
    ]
    return pl.pallas_call(
        kernel,
        out_shape=jax.ShapeDtypeStruct((tok, 8 * hd), BF16),
        in_specs=[any_space] * 5,
        out_specs=any_space,
        scratch_shapes=scratch,
        compiler_params=pltpu.CompilerParams(
            collective_id=0, has_side_effects=True, vmem_limit_bytes=40 * 1024 * 1024
        ),
        cost_estimate=pl.CostEstimate(flops=2_000_000_000, bytes_accessed=4_400_000, transcendentals=0),
    )(queries, keys, values, level_weights, norm_gain.reshape(1, -1))


def solution(mesh):
    return jax.shard_map(
        local,
        mesh=mesh,
        in_specs=(
            P("seq", "head"),
            P("seq", "head"),
            P("seq", "head"),
            P(None, "head", "seq"),
            P("head"),
        ),
        out_specs=P("seq", "head"),
        check_vma=False,
    )
```

time: 166 us -> 54.4 us (0.33)
  the two profiles are of different devices: /device:TPU:120 before, /device:TPU:1 now
where the time goes in v1:
time: 54.4 us; the launch traced here: 54.1 us
  Pallas kernels  47.9 us (88%)
  local copies, waits for them, and re-layouts  6.24 us (11%)
    pallas_call x1, Pallas kernels, local(): pl.pallas_call(kernel, out_shape=jax.ShapeDtypeStruct((tok, 8 * hd), BF16...  47.9 us
    unnamed x11, local copies, waits for them, and re-layouts  6.24 us

profile of v1, /device:TPU:1, one launch (start us, length us, event | category | flops | bytes accessed | tf_op | source)
XLA Modules:
  0.0 54.1 jit_solution(3031861056011173847)
XLA Ops:
  0.0 0.0 copy-start
  0.0 1.2 %copy-done = bf16[512,1024]{1,0:T(8,128)(2,1)S(1)} copy-done((bf16[512,1024]{1,0:T(8,128)(2,1)S(1)}, bf16[512,1024]{1,0:T(8,128)(2,1)}, u32[]{:S(2)}) %copy-start) | copy-done | bytes 1048600
  1.2 0.0 copy-start.1
  1.2 1.2 %copy-done.1 = bf16[512,1024]{1,0:T(8,128)(2,1)S(1)} copy-done((bf16[512,1024]{1,0:T(8,128)(2,1)S(1)}, bf16[512,1024]{1,0:T(8,128)(2,1)}, u32[]{:S(2)}) %copy-start.1) | copy-done | bytes 1048600
  2.5 0.0 copy-start.2
  2.5 1.2 %copy-done.2 = bf16[512,1024]{1,0:T(8,128)(2,1)S(1)} copy-done((bf16[512,1024]{1,0:T(8,128)(2,1)S(1)}, bf16[512,1024]{1,0:T(8,128)(2,1)}, u32[]{:S(2)}) %copy-start.2) | copy-done | bytes 1048600
  3.7 0.0 copy-start.3
  3.7 0.9 %copy-done.3 = f32[9,8,512]{2,1,0:T(8,128)S(1)} copy-done((f32[9,8,512]{2,1,0:T(8,128)S(1)}, f32[9,8,512]{2,1,0:T(8,128)}, u32[]{:S(2)}) %copy-start.3) | copy-done | bytes 147480
  4.6 0.0 copy-start.4
  4.6 0.7 %copy-done.4 = f32[1024]{0:T(1024)S(1)} copy-done((f32[1024]{0:T(1024)S(1)}, f32[1024]{0:T(1024)}, u32[]{:S(2)}) %copy-start.4) | copy-done | bytes 4120
  5.3 47.9 %shard_map.55 = bf16[512,1024]{1,0:T(8,128)(2,1)S(1)} custom-call(bf16[512,1024]{1,0:T(8,128)(2,1)S(1)} %copy-done, bf16[512,1024]{1,0:T(8,128)(2,1)S(1)} %copy-done.1, bf16[512,1024]{1,0:T(8,128)(2,1)S(1)} %copy-done.2, f32[9,8,512]{2,1,0:T(8,128)S(1)} %copy-done.3, f32[1,1024]{1,0:T(1,128)S(1)} %bitcast.1), custom_call_target="tpu_custom_call" | custom-call | flops 2000000000 | bytes 4400000 | tf_op jit(solution)/shard_map/pallas_call | solution.py:407
  53.2 1.0 %copy.7 = bf16[512,1024]{1,0:T(8,128)(2,1)} copy(bf16[512,1024]{1,0:T(8,128)(2,1)S(1)} %shard_map.55) | data formatting | bytes 2097152
Async XLA Ops:
  0.0 1.2 %copy-start = (bf16[512,1024]{1,0:T(8,128)(2,1)S(1)}, bf16[512,1024]{1,0:T(8,128)(2,1)}, u32[]{:S(2)}) copy-start(bf16[512,1024]{1,0:T(8,128)(2,1)} %q_hbm.1) | copy-start | bytes 3145732
  1.2 1.2 %copy-start.1 = (bf16[512,1024]{1,0:T(8,128)(2,1)S(1)}, bf16[512,1024]{1,0:T(8,128)(2,1)}, u32[]{:S(2)}) copy-start(bf16[512,1024]{1,0:T(8,128)(2,1)} %k_hbm.1) | copy-start | bytes 3145732
  2.5 1.2 %copy-start.2 = (bf16[512,1024]{1,0:T(8,128)(2,1)S(1)}, bf16[512,1024]{1,0:T(8,128)(2,1)}, u32[]{:S(2)}) copy-start(bf16[512,1024]{1,0:T(8,128)(2,1)} %v_hbm.1) | copy-start | bytes 3145732
  3.7 0.9 %copy-start.3 = (f32[9,8,512]{2,1,0:T(8,128)S(1)}, f32[9,8,512]{2,1,0:T(8,128)}, u32[]{:S(2)}) copy-start(f32[9,8,512]{2,1,0:T(8,128)} %w_hbm.1) | copy-start | bytes 442372
  4.6 0.7 %copy-start.4 = (f32[1024]{0:T(1024)S(1)}, f32[1024]{0:T(1024)}, u32[]{:S(2)}) copy-start(f32[1024]{0:T(1024)} %param.9) | copy-start | bytes 12292

commit v2 on v1

v2 whole, which is shorter than its diff:
```python
import jax
import jax.numpy as jnp
from jax import lax
from jax.experimental import pallas as pl
from jax.experimental.pallas import tpu as pltpu
from jax.sharding import PartitionSpec as P

HEAD_DIM = 128
STRETCH = 256
D = 4096
EPSILON = 1e-06

RING = 8
COLS = 4
HEADS_HERE = 8
TOK = 512
EARLY = 5
HALF = 64
FAR_FIRST = (4, 3, 5, 2, 6, 1, 7)
NEAR_FIRST = (1, 7, 2, 6, 3, 5, 4)
PAIRS = ((0, 1), (0, 2), (1, 2), (2, 3), (0, 4), (1, 4), (2, 4), (3, 4), (4, 5), (4, 6), (5, 6), (6, 7))
MESH = pl.DeviceIdType.MESH
F32 = jnp.float32
BF16 = jnp.bfloat16


def nt(a, b):
    return lax.dot_general(a, b, (((1,), (1,)), ((), ())), preferred_element_type=F32)


def tn(a, b):
    return lax.dot_general(a, b, (((0,), (0,)), ((), ())), preferred_element_type=F32)


def nn(a, b):
    return jnp.dot(a, b, preferred_element_type=F32)


def kernel(
    q_hbm, k_hbm, v_hbm, w_hbm, g_hbm, out_hbm,
    q_s, k_s, v_s, w_v, g_v, w_rows, w_cols, out_s,
    first, own_sum, own_bf, pair_in, core0, chip_sum, ring_in, ring_sum, totals, low, high,
    acc, sq, sq_in,
    load_sem, misc_sem, out_sem, ready,
    pair_send, pair_recv, core_send, core_recv, ring_send, ring_recv, next_send, next_recv,
    low_send, low_recv, tot_send, tot_recv, high_send, high_recv, up_send, up_recv,
    fwl_send, fwl_recv, fwh_send, fwh_recv, sq_send, sq_recv,
):
    seq = lax.axis_index("seq")
    col = lax.axis_index("head")
    core = lax.rem(seq, 2)
    y = lax.rem(seq // 2, RING)
    z = seq // (2 * RING)
    y_bits = (lax.rem(y, 2) == 1, lax.rem(y // 2, 2) == 1, y // 4 == 1)
    z_bits = (lax.rem(z, 2) == 1, lax.rem(z // 2, 2) == 1, z // 4 == 1)
    sent = []

    def device(z_, y_, core_):
        return (z_ * (2 * RING) + y_ * 2 + core_, col)

    sibling = device(z, y, 1 - core)
    mine = pl.ds(pl.multiple_of(core * HALF, HALF), HALF)
    other = pl.ds(pl.multiple_of((1 - core) * HALF, HALF), HALF)

    def row_peer(d):
        return lax.rem(y + d, RING)

    def remote(src, dst, send, recv, target):
        return pltpu.make_async_remote_copy(
            src_ref=src, dst_ref=dst, send_sem=send, recv_sem=recv, device_id=target, device_id_type=MESH
        )

    def when(cond, f):
        if cond is None:
            f()
        else:
            pl.when(cond)(f)

    def launch(copy, cond=None):
        when(cond, copy.start)
        sent.append((cond, copy))

    def finish():
        for cond, copy in sent:
            when(cond, copy.wait_send)

    order = FAR_FIRST + (0,)
    loads = {}
    for name, src, dst, slot in (("k", k_hbm, k_s, 0), ("v", v_hbm, v_s, 1), ("q", q_hbm, q_s, 2)):
        for i, d in enumerate(order):
            h = row_peer(d)
            columns = pl.ds(pl.multiple_of(h * HEAD_DIM, HEAD_DIM), HEAD_DIM)
            loads[name, i] = pltpu.make_async_copy(src.at[:, columns], dst.at[h], load_sem.at[slot, i])
    for i in range(HEADS_HERE):
        loads["k", i].start()
        loads["v", i].start()
    w_load = pltpu.make_async_copy(w_hbm, w_v, misc_sem.at[0])
    g_load = pltpu.make_async_copy(g_hbm, g_v, misc_sem.at[1])

    barrier = pltpu.get_barrier_semaphore()

    def greet(target):
        pl.semaphore_signal(barrier, inc=1, device_id=target, device_id_type=MESH)

    for a, b in PAIRS:
        pl.when(z == a)(lambda: greet(device(b, y, core)))
    greet(sibling)
    for d in range(1, RING):
        greet(device(z, row_peer(d), core))
    for d in range(1, COLS):
        greet((seq, lax.rem(col + d, COLS)))

    for h in range(HEADS_HERE):
        loads["q", h].start()
    w_load.start()
    g_load.start()
    for level in range(3):

        @pl.when(jnp.logical_not(z_bits[level]))
        def _():
            high[:, mine, level * 128 : (level + 1) * 128] = jnp.zeros((HEADS_HERE, HALF, HEAD_DIM), BF16)

    to_sibling = []
    for i, d in enumerate(order):
        h = row_peer(d)
        to_sibling.append(
            remote(own_sum.at[h, other, :], pair_in.at[h], pair_send.at[i], pair_recv.at[i], sibling)
        )
    for i, d in enumerate(order):
        h = row_peer(d)
        loads["k", i].wait()
        loads["v", i].wait()
        k = k_s[h]
        v = v_s[h]
        s0 = tn(k[:STRETCH], v[:STRETCH])
        s1 = tn(k[STRETCH:], v[STRETCH:])
        first[h] = s0.astype(BF16)
        s = s0 + s1
        own_sum[h] = s
        own_bf[h] = s.astype(BF16)
        if i == 0:
            for row in range(RING):
                rows_in = [a for a, b in PAIRS if b == row]

                @pl.when(z == row)
                def _():
                    pl.semaphore_wait(barrier, 1 + RING - 1 + COLS - 1 + len(rows_in))
                    for a in rows_in:
                        pl.semaphore_signal(
                            ready.at[row], inc=1, device_id=device(a, y, core), device_id_type=MESH
                        )

        launch(to_sibling[i])

    to_core1 = remote(own_bf, core0, core_send, core_recv, sibling)
    launch(to_core1, core == 0)

    def to_owner(d):
        h = row_peer(d)
        return remote(chip_sum.at[h], ring_in.at[y], ring_send.at[d - 1], ring_recv.at[d - 1], device(z, h, core))

    for i, d in enumerate(order):
        h = row_peer(d)
        to_sibling[i].wait_recv()
        c = (own_sum[h, mine, :] + pair_in[h]).astype(BF16)
        chip_sum[h] = c
        if d:
            launch(to_owner(d))
        else:
            ring_in[y] = c

    w_load.wait()
    for h in range(HEADS_HERE):
        for level in range(9):
            w_rows[h, level : level + 1, :] = w_v[level, h : h + 1, :]
        w_rows[h, 9:16, :] = jnp.zeros((7, TOK), F32)
    for h in range(HEADS_HERE):
        w_cols[h] = w_rows[h].T

    for h in range(HEADS_HERE):
        loads["q", h].wait()

    causal = lax.broadcasted_iota(jnp.int32, (STRETCH, STRETCH), 0) >= lax.broadcasted_iota(
        jnp.int32, (STRETCH, STRETCH), 1
    )

    def within(h):
        for s in range(2):
            rows = slice(s * STRETCH, (s + 1) * STRETCH)
            qs = q_s[h, rows, :]
            probs = jnp.where(causal, nt(qs, k_s[h, rows, :]), 0.0).astype(BF16)
            part = w_cols[h, rows, 0:1] * nn(probs, v_s[h, rows, :])
            if s == 1:
                part += w_cols[h, rows, 1:2] * nn(qs, first[h])
            acc[h, rows, :] = part

    for h in range(0, EARLY):
        within(h)

    to_next = remote(
        chip_sum, low.at[0, :, mine, :], next_send, next_recv, device(z, lax.rem(y + 1, RING), core)
    )
    launch(to_next, jnp.logical_not(y_bits[0]))

    for d in range(1, RING):
        to_owner(d).wait_recv()
    part = [ring_in[j].astype(F32) for j in range(RING)]
    s01 = part[0] + part[1]
    s0123 = s01 + (part[2] + part[3])
    s45 = part[4] + part[5]
    totals[z] = s0123 + (s45 + (part[6] + part[7]))

    for a, b in PAIRS:

        @pl.when(z == a)
        def _():
            pl.semaphore_wait(ready.at[b], 1)

        launch(
            remote(totals.at[a], totals.at[a], tot_send.at[b], tot_recv.at[a], device(b, y, core)), z == a
        )

    ring_sum[0] = s01.astype(BF16)
    ring_sum[1] = s45.astype(BF16)
    ring_sum[2] = s0123.astype(BF16)

    for h in range(EARLY, HEADS_HERE):
        within(h)

    level_lanes = [slice(level * 128, (level + 1) * 128) for level in range(3)]
    for row in range(1, RING):
        rows_in = [a for a, b in PAIRS if b == row]
        level = len(rows_in).bit_length() - 1

        @pl.when(z == row)
        def _():
            for a in rows_in:
                remote(totals.at[a], totals.at[a], tot_send.at[row], tot_recv.at[a], device(row, y, core)).wait_recv()
            state = totals[rows_in[0]]
            for a in rows_in[1:]:
                state = state + totals[a]
            high[y, mine, level_lanes[level]] = state.astype(BF16)

    lowest = (1 - lax.rem(z, 2)) * (2 - lax.rem(z // 2, 2))
    lanes = pl.ds(pl.multiple_of(lowest * 128, 128), 128)

    def along_row(d):
        return remote(
            high.at[y, mine, lanes], high.at[y, mine, lanes], high_send.at[d - 1], high_recv.at[d - 1],
            device(z, row_peer(d), core),
        )

    for d in FAR_FIRST:
        launch(along_row(d), z > 0)

    def low_copy(level, d):
        target = row_peer(d)
        src = ring_sum.at[target // 4] if level == 1 else ring_sum.at[2]
        return remote(
            src, low.at[level, y, mine, :], low_send.at[level - 1, d - 1], low_recv.at[level - 1, d - 1],
            device(z, target, core),
        )

    for d in FAR_FIRST:
        target = row_peer(d)
        launch(low_copy(1, d), lax.rem(target // 2, 2) == 1)
        launch(low_copy(2, d), target // 4 == 1)

    @pl.when(y_bits[1])
    def _():
        low[1, y, mine, :] = ring_sum[y // 4]

    @pl.when(y_bits[2])
    def _():
        low[2, y, mine, :] = ring_sum[2]

    @pl.when(core == 1)
    def _():
        to_core1.wait_recv()
        for h in range(HEADS_HERE):
            acc[h] += w_cols[h, :, 2:3] * nn(q_s[h], core0[h])

    def share_low(level):
        return remote(
            low.at[level, :, mine, :], low.at[level, :, mine, :], fwl_send.at[level], fwl_recv.at[level], sibling
        )

    def low_arrivals():
        for level in range(3):

            @pl.when(y_bits[level])
            def _():
                if level == 0:
                    to_next.wait_recv()
                else:
                    for d in range(1, RING):
                        low_copy(level, d).wait_recv()
                share_low(level).start()

        for level in range(3):

            @pl.when(y_bits[level])
            def _():
                share_low(level).wait_recv()
                for h in range(HEADS_HERE):
                    acc[h] += w_cols[h, :, 3 + level : 4 + level] * nn(q_s[h], low[level, h])

    for level in range(3):
        sent.append((y_bits[level], share_low(level)))

    pl.when(z == RING - 1)(low_arrivals)

    def share_high(i, h):
        return remote(high.at[h, mine, :], high.at[h, mine, :], fwh_send.at[i], fwh_recv.at[i], sibling)

    def upward(level, i, h):
        ref = high.at[h, mine, level_lanes[level]]
        return remote(ref, ref, up_send.at[level - 1, i], up_recv.at[level - 1, i], device(lax.rem(z + 1, RING), y, core))

    arrivals = (0,) + NEAR_FIRST
    from_below = {1: lax.rem(z, 4) == 3, 2: z > 4}
    go_up = {1: lax.rem(z, 4) == 2, 2: jnp.logical_and(z >= 4, z < 7)}
    for i, d in enumerate(arrivals):
        h = lax.rem(y + RING - d, RING)
        for level in (2, 1):
            pl.when(from_below[level])(upward(level, i, h).wait_recv)
        if d:
            pl.when(z > 0)(along_row(d).wait_recv)
        for level in (2, 1):
            launch(upward(level, i, h), go_up[level])
        launch(share_high(i, h))

    pl.when(z < RING - 1)(low_arrivals)

    sq[...] = jnp.zeros_like(sq)
    for i, d in enumerate(arrivals):
        h = lax.rem(y + RING - d, RING)
        share_high(i, h).wait_recv()
        r = nn(q_s[h], high[h])
        a = acc[h]
        for level in range(3):
            a += w_cols[h, :, 6 + level : 7 + level] * r[:, level_lanes[level]]
        acc[h] = a
        sq[...] += a * a

    sq_in[col, 0:1, :] = jnp.sum(sq[...].T, axis=0, keepdims=True)

    def to_cols(d):
        return remote(
            sq_in.at[col, 0:1], sq_in.at[col, 0:1], sq_send.at[d - 1], sq_recv.at[d - 1],
            (seq, lax.rem(col + d, COLS)),
        )

    for d in (2, 1, 3):
        launch(to_cols(d))
    g_load.wait()
    for d in (1, 3, 2):
        to_cols(d).wait_recv()
    squares = (sq_in[0, 0:1, :] + sq_in[1, 0:1, :]) + (sq_in[2, 0:1, :] + sq_in[3, 0:1, :])
    inverse = lax.rsqrt(squares / D + EPSILON)
    scale = jnp.broadcast_to(inverse, (HEAD_DIM, TOK)).T

    def store(h):
        columns = pl.ds(h * HEAD_DIM, HEAD_DIM)
        return pltpu.make_async_copy(out_s.at[h], out_hbm.at[:, columns], out_sem.at[h])

    for h in range(HEADS_HERE):
        out_s[h] = (acc[h] * scale * g_v[:, h * HEAD_DIM : (h + 1) * HEAD_DIM]).astype(BF16)
        store(h).start()
    finish()
    for h in range(HEADS_HERE):
        store(h).wait()


def local(queries, keys, values, level_weights, norm_gain):
    hd, tok, half, ring = HEAD_DIM, TOK, HALF, RING
    dma = pltpu.SemaphoreType.DMA
    any_space = pl.BlockSpec(memory_space=pl.ANY)
    scratch = [
        pltpu.VMEM((8, tok, hd), BF16),
        pltpu.VMEM((8, tok, hd), BF16),
        pltpu.VMEM((8, tok, hd), BF16),
        pltpu.VMEM((9, 8, tok), F32),
        pltpu.VMEM((1, 1024), F32),
        pltpu.VMEM((8, 16, tok), F32),
        pltpu.VMEM((8, tok, 16), F32),
        pltpu.VMEM((8, tok, hd), BF16),
        pltpu.VMEM((8, hd, hd), BF16),
        pltpu.VMEM((8, hd, hd), F32),
        pltpu.VMEM((8, hd, hd), BF16),
        pltpu.VMEM((8, half, hd), F32),
        pltpu.VMEM((8, hd, hd), BF16),
        pltpu.VMEM((8, half, hd), BF16),
        pltpu.VMEM((ring, half, hd), BF16),
        pltpu.VMEM((3, half, hd), BF16),
        pltpu.VMEM((ring, half, hd), F32),
        pltpu.VMEM((3, 8, hd, hd), BF16),
        pltpu.VMEM((8, hd, 3 * hd), BF16),
        pltpu.VMEM((8, tok, hd), F32),
        pltpu.VMEM((tok, hd), F32),
        pltpu.VMEM((COLS, 8, tok), F32),
        dma((3, 8)), dma((2,)), dma((8,)), pltpu.SemaphoreType.REGULAR((8,)),
        dma((8,)), dma((8,)), dma, dma, dma((7,)), dma((7,)), dma, dma,
        dma((2, 7)), dma((2, 7)), dma((8,)), dma((8,)), dma((7,)), dma((7,)), dma((2, 8)), dma((2, 8)),
        dma((3,)), dma((3,)), dma((8,)), dma((8,)), dma((3,)), dma((3,)),
    ]
    return pl.pallas_call(
        kernel,
        out_shape=jax.ShapeDtypeStruct((tok, 8 * hd), BF16),
        in_specs=[any_space] * 5,
        out_specs=any_space,
        scratch_shapes=scratch,
        compiler_params=pltpu.CompilerParams(
            collective_id=0, has_side_effects=True, vmem_limit_bytes=60 * 1024 * 1024
        ),
        cost_estimate=pl.CostEstimate(flops=2_000_000_000, bytes_accessed=4_400_000, transcendentals=0),
    )(queries, keys, values, level_weights, norm_gain.reshape(1, -1))


def solution(mesh):
    return jax.shard_map(
        local,
        mesh=mesh,
        in_specs=(
            P("seq", "head"),
            P("seq", "head"),
            P("seq", "head"),
            P(None, "head", "seq"),
            P("head"),
        ),
        out_specs=P("seq", "head"),
        check_vma=False,
    )
```

time: 54.4 us -> 41.7 us (0.77)
  the two profiles are of different devices: /device:TPU:1 before, /device:TPU:448 now
where the time goes in v2:
time: 41.7 us; the launch traced here: 41.6 us
  Pallas kernels  39.3 us (94%)
  local copies, waits for them, and re-layouts  2.26 us (5%)
    pallas_call x1, Pallas kernels, local(): pl.pallas_call(kernel, out_shape=jax.ShapeDtypeStruct((tok, 8 * hd), BF16...  39.3 us
    unnamed x1, local copies, waits for them, and re-layouts  2.26 us

profile of v2, /device:TPU:448, one launch (start us, length us, event | category | flops | bytes accessed | tf_op | source)
XLA Modules:
  0.0 41.6 jit_solution(806179339760705054)
XLA Ops:
  0.0 39.3 %shard_map.55 = bf16[512,1024]{1,0:T(8,128)(2,1)} custom-call(bf16[512,1024]{1,0:T(8,128)(2,1)} %q_hbm.1, bf16[512,1024]{1,0:T(8,128)(2,1)} %k_hbm.1, bf16[512,1024]{1,0:T(8,128)(2,1)} %v_hbm.1, f32[9,8,512]{2,1,0:T(8,128)} %w_hbm.1, f32[1,1024]{1,0:T(1,128)} %bitcast.1), custom_call_target="tpu_custom_call" | custom-call | flops 2000000000 | bytes 4400000 | tf_op jit(solution)/shard_map/pallas_call | solution.py:407
  39.3 2.3 %copy.7 = bf16[512,1024]{1,0:T(8,128)(2,1)} copy(bf16[512,1024]{1,0:T(8,128)(2,1)} %shard_map.55) | data formatting | bytes 2097152

commit v3 on v2

v3 whole, which is shorter than its diff:
```python
import jax
import jax.numpy as jnp
from jax import lax
from jax.experimental import pallas as pl
from jax.experimental.pallas import tpu as pltpu
from jax.sharding import PartitionSpec as P

HEAD_DIM = 128
STRETCH = 256
D = 4096
EPSILON = 1e-06

RING = 8
COLS = 4
HEADS_HERE = 8
TOK = 512
EARLY = 5
HALF = 64
FAR_FIRST = (4, 3, 5, 2, 6, 1, 7)
NEAR_FIRST = (1, 7, 2, 6, 3, 5, 4)
PAIRS = ((0, 1), (0, 2), (1, 2), (2, 3), (0, 4), (1, 4), (2, 4), (3, 4), (4, 5), (4, 6), (5, 6), (6, 7))
TARGETS = {a: [b for c, b in PAIRS if c == a] for a in range(RING - 1)}
MESH = pl.DeviceIdType.MESH
F32 = jnp.float32
BF16 = jnp.bfloat16


def nt(a, b):
    return lax.dot_general(a, b, (((1,), (1,)), ((), ())), preferred_element_type=F32)


def tn(a, b):
    return lax.dot_general(a, b, (((0,), (0,)), ((), ())), preferred_element_type=F32)


def nn(a, b):
    return jnp.dot(a, b, preferred_element_type=F32)


def kernel(
    q_hbm, k_hbm, v_hbm, w_hbm, g_hbm, out,
    q_s, kv_s, w_v, g_v, w_rows, w_cols,
    first, own_sum, own_bf, pair_in, core0, chip_sum, ring_in, ring_sum, totals, low, high,
    acc, sq, sq_in,
    load_sem, misc_sem, ready,
    pair_send, pair_recv, core_send, core_recv, ring_send, ring_recv, next_send, next_recv,
    low_send, low_recv, tot_send, tot_recv, high_send, high_recv, up_send, up_recv,
    fwl_send, fwl_recv, fwh_send, fwh_recv, sq_send, sq_recv,
):
    seq = lax.axis_index("seq")
    col = lax.axis_index("head")
    core = lax.rem(seq, 2)
    y = lax.rem(seq // 2, RING)
    z = seq // (2 * RING)
    y_bits = (lax.rem(y, 2) == 1, lax.rem(y // 2, 2) == 1, y // 4 == 1)
    z_bits = (lax.rem(z, 2) == 1, lax.rem(z // 2, 2) == 1, z // 4 == 1)
    ends = []

    def device(z_, y_, core_):
        return (z_ * (2 * RING) + y_ * 2 + core_, col)

    sibling = device(z, y, 1 - core)
    mine = pl.ds(pl.multiple_of(core * HALF, HALF), HALF)
    other = pl.ds(pl.multiple_of((1 - core) * HALF, HALF), HALF)

    def row_peer(d):
        return lax.rem(y + d, RING)

    def remote(src, dst, send, recv, target):
        return pltpu.make_async_remote_copy(
            src_ref=src, dst_ref=dst, send_sem=send, recv_sem=recv, device_id=target, device_id_type=MESH
        )

    def when(cond, f):
        if cond is None:
            f()
        else:
            pl.when(cond)(f)

    def launch(copy, cond=None, alone=True):
        when(cond, copy.start)
        if alone:
            ends.append((cond, copy))

    def finish():
        for cond, copy in ends:
            when(cond, copy.wait_send)

    order = FAR_FIRST + (0,)

    def columns_of(i):
        return pl.ds(pl.multiple_of(row_peer(order[i]) * HEAD_DIM, HEAD_DIM), HEAD_DIM)

    for i, d in enumerate(order):
        pltpu.make_async_copy(k_hbm.at[:, columns_of(i)], kv_s.at[row_peer(d), 0], load_sem.at[i]).start()
        pltpu.make_async_copy(v_hbm.at[:, columns_of(i)], kv_s.at[row_peer(d), 1], load_sem.at[i]).start()
    w_load = pltpu.make_async_copy(w_hbm, w_v, misc_sem.at[0])
    g_load = pltpu.make_async_copy(g_hbm, g_v, misc_sem.at[1])

    barrier = pltpu.get_barrier_semaphore()

    def greet(target):
        pl.semaphore_signal(barrier, inc=1, device_id=target, device_id_type=MESH)

    for d in FAR_FIRST:
        greet(device(z, row_peer(d), core))
    for a, b in PAIRS:
        pl.when(z == a)(lambda: greet(device(b, y, core)))
    greet(sibling)
    for d in range(1, COLS):
        greet((seq, lax.rem(col + d, COLS)))

    for i, d in enumerate(order):
        pltpu.make_async_copy(q_hbm.at[:, columns_of(i)], q_s.at[row_peer(d)], misc_sem.at[2]).start()
    w_load.start()
    g_load.start()
    for level in range(3):

        @pl.when(jnp.logical_not(z_bits[level]))
        def _():
            high[:, mine, level * 128 : (level + 1) * 128] = jnp.zeros((HEADS_HERE, HALF, HEAD_DIM), BF16)

    to_sibling = []
    for i, d in enumerate(order):
        h = row_peer(d)
        to_sibling.append(
            remote(own_sum.at[h, other, :], pair_in.at[h], pair_send, pair_recv.at[i], sibling)
        )
    for i, d in enumerate(order):
        h = row_peer(d)
        pltpu.make_async_copy(kv_s.at[h], kv_s.at[h], load_sem.at[i]).wait()
        k = kv_s[h, 0]
        v = kv_s[h, 1]
        s0 = tn(k[:STRETCH], v[:STRETCH])
        s1 = tn(k[STRETCH:], v[STRETCH:])
        first[h] = s0.astype(BF16)
        s = s0 + s1
        own_sum[h] = s
        own_bf[h] = s.astype(BF16)
        if i == 0:
            for row in range(RING):
                rows_in = [a for a, b in PAIRS if b == row]

                @pl.when(z == row)
                def _():
                    pl.semaphore_wait(barrier, 1 + RING - 1 + COLS - 1 + len(rows_in))
                    for a in rows_in:
                        pl.semaphore_signal(
                            ready.at[TARGETS[a].index(row)], inc=1, device_id=device(a, y, core), device_id_type=MESH
                        )

        launch(to_sibling[i], alone=False)

    ends.append((None, remote(own_sum.at[:, other, :], pair_in, pair_send, pair_recv.at[0], sibling)))
    to_core1 = remote(own_bf, core0, core_send, core_recv, sibling)
    launch(to_core1, core == 0)

    def to_owner(d):
        h = row_peer(d)
        return remote(chip_sum.at[h], ring_in.at[y], ring_send, ring_recv, device(z, h, core))

    for i, d in enumerate(order):
        h = row_peer(d)
        to_sibling[i].wait_recv()
        c = (own_sum[h, mine, :] + pair_in[h]).astype(BF16)
        chip_sum[h] = c
        if d:
            launch(to_owner(d), alone=False)
        else:
            ring_in[y] = c

    def row_total(count, send, recv):
        return remote(chip_sum.at[0:count], ring_in.at[0:count], send, recv, device(z, row_peer(1), core))

    from_row = row_total(RING - 1, ring_send, ring_recv)
    ends.append((None, from_row))

    w_load.wait()
    for h in range(HEADS_HERE):
        for level in range(9):
            w_rows[h, level : level + 1, :] = w_v[level, h : h + 1, :]
        w_rows[h, 9:16, :] = jnp.zeros((7, TOK), F32)
    for h in range(HEADS_HERE):
        w_cols[h] = w_rows[h].T

    pltpu.make_async_copy(q_s, q_s, misc_sem.at[2]).wait()

    causal = lax.broadcasted_iota(jnp.int32, (STRETCH, STRETCH), 0) >= lax.broadcasted_iota(
        jnp.int32, (STRETCH, STRETCH), 1
    )

    def within(h):
        for s in range(2):
            rows = slice(s * STRETCH, (s + 1) * STRETCH)
            qs = q_s[h, rows, :]
            probs = jnp.where(causal, nt(qs, kv_s[h, 0, rows, :]), 0.0).astype(BF16)
            part = w_cols[h, rows, 0:1] * nn(probs, kv_s[h, 1, rows, :])
            if s == 1:
                part += w_cols[h, rows, 1:2] * nn(qs, first[h])
            acc[h, rows, :] = part

    for h in range(0, EARLY):
        within(h)

    to_next = remote(
        chip_sum, low.at[0, :, mine, :], next_send, next_recv, device(z, lax.rem(y + 1, RING), core)
    )
    launch(to_next, jnp.logical_not(y_bits[0]))

    from_row.wait_recv()
    part = [ring_in[j].astype(F32) for j in range(RING)]
    s01 = part[0] + part[1]
    s0123 = s01 + (part[2] + part[3])
    s45 = part[4] + part[5]
    totals[z] = s0123 + (s45 + (part[6] + part[7]))

    for a, b in PAIRS:

        @pl.when(z == a)
        def _():
            pl.semaphore_wait(ready.at[TARGETS[a].index(b)], 1)

        launch(
            remote(
                totals.at[a], totals.at[a], tot_send.at[TARGETS[a].index(b)],
                tot_recv.at[a - b + (b & -b)], device(b, y, core),
            ),
            z == a,
        )

    ring_sum[0] = s01.astype(BF16)
    ring_sum[1] = s45.astype(BF16)
    ring_sum[2] = s0123.astype(BF16)

    def low_copy(level, d):
        target = row_peer(d)
        src = ring_sum.at[target // 4] if level == 1 else ring_sum.at[2]
        return remote(
            src, low.at[level, y, mine, :], low_send.at[level - 1], low_recv.at[level - 1], device(z, target, core)
        )

    for d in FAR_FIRST:
        launch(low_copy(1, d), lax.rem(row_peer(d) // 2, 2) == 1, alone=False)
    for level in (1, 2):
        ends.append((y_bits[level], row_total(3, low_send.at[level - 1], ring_recv)))
        ends.append((jnp.logical_not(y_bits[level]), row_total(4, low_send.at[level - 1], ring_recv)))

    @pl.when(y_bits[1])
    def _():
        low[1, y, mine, :] = ring_sum[y // 4]

    @pl.when(y_bits[2])
    def _():
        low[2, y, mine, :] = ring_sum[2]

    for h in range(EARLY, HEADS_HERE):
        within(h)

    level_lanes = [slice(level * 128, (level + 1) * 128) for level in range(3)]
    for row in range(1, RING):
        rows_in = [a for a, b in PAIRS if b == row]
        level = len(rows_in).bit_length() - 1

        @pl.when(z == row)
        def _():
            for a in rows_in:
                remote(
                    totals.at[a], totals.at[a], tot_send.at[0], tot_recv.at[a - rows_in[0]], device(a, y, core)
                ).wait_recv()
            state = totals[rows_in[0]]
            for a in rows_in[1:]:
                state = state + totals[a]
            high[y, mine, level_lanes[level]] = state.astype(BF16)

    lowest = (1 - lax.rem(z, 2)) * (2 - lax.rem(z // 2, 2))
    lanes = pl.ds(pl.multiple_of(lowest * 128, 128), 128)

    def along_row(d):
        return remote(
            high.at[y, mine, lanes], high.at[y, mine, lanes], high_send, high_recv.at[d - 1],
            device(z, row_peer(d), core),
        )

    for d in FAR_FIRST:
        launch(along_row(d), z > 0, alone=False)

    @pl.when(core == 1)
    def _():
        to_core1.wait_recv()
        for h in range(HEADS_HERE):
            acc[h] += w_cols[h, :, 2:3] * nn(q_s[h], core0[h])

    when(z > 0, row_total(RING - 1, high_send, ring_recv).wait_send)
    for d in FAR_FIRST:
        launch(low_copy(2, d), row_peer(d) // 4 == 1, alone=False)

    def share_low(level):
        return remote(
            low.at[level, :, mine, :], low.at[level, :, mine, :], fwl_send.at[level], fwl_recv.at[level], sibling
        )

    def low_arrivals():
        for level in range(3):

            @pl.when(y_bits[level])
            def _():
                if level == 0:
                    to_next.wait_recv()
                else:
                    row_total(RING - 1, ring_send, low_recv.at[level - 1]).wait_recv()
                share_low(level).start()

        for level in range(3):

            @pl.when(y_bits[level])
            def _():
                share_low(level).wait_recv()
                for h in range(HEADS_HERE):
                    acc[h] += w_cols[h, :, 3 + level : 4 + level] * nn(q_s[h], low[level, h])

    for level in range(3):
        ends.append((y_bits[level], share_low(level)))

    pl.when(z == RING - 1)(low_arrivals)

    def share_high(i, h):
        return remote(high.at[h, mine, :], high.at[h, mine, :], fwh_send, fwh_recv.at[i], sibling)

    def upward(level, i, h):
        ref = high.at[h, mine, level_lanes[level]]
        return remote(ref, ref, up_send.at[level - 1], up_recv.at[level - 1, i], device(lax.rem(z + 1, RING), y, core))

    arrivals = (0,) + NEAR_FIRST
    from_below = {1: lax.rem(z, 4) == 3, 2: z > 4}
    go_up = {1: lax.rem(z, 4) == 2, 2: jnp.logical_and(z >= 4, z < 7)}
    for i, d in enumerate(arrivals):
        h = lax.rem(y + RING - d, RING)
        for level in (2, 1):
            pl.when(from_below[level])(upward(level, i, h).wait_recv)
        if d:
            pl.when(z > 0)(along_row(d).wait_recv)
        for level in (2, 1):
            launch(upward(level, i, h), go_up[level], alone=False)
        launch(share_high(i, h), alone=False)

    whole = high.at[:, mine, :]
    ends.append((None, remote(whole, whole, fwh_send, fwh_recv.at[0], sibling)))
    for level in (1, 2):
        ends.append((go_up[level], row_total(RING, up_send.at[level - 1], ring_recv)))
    pl.when(z < RING - 1)(low_arrivals)

    sq[...] = jnp.zeros_like(sq)
    for i, d in enumerate(arrivals):
        h = lax.rem(y + RING - d, RING)
        share_high(i, h).wait_recv()
        r = nn(q_s[h], high[h])
        a = acc[h]
        for level in range(3):
            a += w_cols[h, :, 6 + level : 7 + level] * r[:, level_lanes[level]]
        acc[h] = a
        sq[...] += a * a

    sq_in[col, 0:1, :] = jnp.sum(sq[...].T, axis=0, keepdims=True)

    def to_cols(d):
        return remote(
            sq_in.at[col, 0:1], sq_in.at[col, 0:1], sq_send, sq_recv,
            (seq, lax.rem(col + d, COLS)),
        )

    for d in (2, 1, 3):
        launch(to_cols(d), alone=False)
    g_load.wait()
    others = sq_in.at[0 : COLS - 1, 0:1]
    from_cols = remote(others, others, sq_send, sq_recv, (seq, lax.rem(col + 1, COLS)))
    ends.append((None, from_cols))
    from_cols.wait_recv()
    squares = (sq_in[0, 0:1, :] + sq_in[1, 0:1, :]) + (sq_in[2, 0:1, :] + sq_in[3, 0:1, :])
    inverse = lax.rsqrt(squares / D + EPSILON)
    scale = jnp.broadcast_to(inverse, (HEAD_DIM, TOK)).T

    for h in range(HEADS_HERE):
        columns = slice(h * HEAD_DIM, (h + 1) * HEAD_DIM)
        out[:, columns] = (acc[h] * scale * g_v[:, columns]).astype(BF16)
    finish()


def local(queries, keys, values, level_weights, norm_gain):
    hd, tok, half, ring = HEAD_DIM, TOK, HALF, RING
    dma = pltpu.SemaphoreType.DMA
    any_space = pl.BlockSpec(memory_space=pl.ANY)
    scratch = [
        pltpu.VMEM((8, tok, hd), BF16),
        pltpu.VMEM((8, 2, tok, hd), BF16),
        pltpu.VMEM((9, 8, tok), F32),
        pltpu.VMEM((1, 1024), F32),
        pltpu.VMEM((8, 16, tok), F32),
        pltpu.VMEM((8, tok, 16), F32),
        pltpu.VMEM((8, hd, hd), BF16),
        pltpu.VMEM((8, hd, hd), F32),
        pltpu.VMEM((8, hd, hd), BF16),
        pltpu.VMEM((8, half, hd), F32),
        pltpu.VMEM((8, hd, hd), BF16),
        pltpu.VMEM((8, half, hd), BF16),
        pltpu.VMEM((ring, half, hd), BF16),
        pltpu.VMEM((3, half, hd), BF16),
        pltpu.VMEM((ring, half, hd), F32),
        pltpu.VMEM((3, 8, hd, hd), BF16),
        pltpu.VMEM((8, hd, 3 * hd), BF16),
        pltpu.VMEM((8, tok, hd), F32),
        pltpu.VMEM((tok, hd), F32),
        pltpu.VMEM((COLS, 8, tok), F32),
        dma((8,)), dma((3,)), pltpu.SemaphoreType.REGULAR((3,)),
        dma, dma((8,)), dma, dma, dma, dma, dma, dma,
        dma((2,)), dma((2,)), dma((3,)), dma((4,)), dma, dma((7,)), dma((2,)), dma((2, 8)),
        dma((3,)), dma((3,)), dma, dma((8,)), dma, dma,
    ]
    return pl.pallas_call(
        kernel,
        out_shape=pltpu.VMEM((tok, 8 * hd), BF16),
        in_specs=[any_space] * 5,
        out_specs=pl.BlockSpec(memory_space=pltpu.VMEM),
        scratch_shapes=scratch,
        compiler_params=pltpu.CompilerParams(
            collective_id=0, has_side_effects=True, vmem_limit_bytes=60 * 1024 * 1024
        ),
        cost_estimate=pl.CostEstimate(flops=2_000_000_000, bytes_accessed=4_400_000, transcendentals=0),
    )(queries, keys, values, level_weights, norm_gain.reshape(1, -1))


def solution(mesh):
    return jax.shard_map(
        local,
        mesh=mesh,
        in_specs=(
            P("seq", "head"),
            P("seq", "head"),
            P("seq", "head"),
            P(None, "head", "seq"),
            P("head"),
        ),
        out_specs=P("seq", "head"),
        check_vma=False,
    )
```

time: 41.7 us -> 38.5 us (0.923)
  Pallas kernels: 39.3 us -> 37.3 us
  local copies, waits for them, and re-layouts: 2.26 us -> 0.97 us
    pallas_call x1, Pallas kernels: 39.3 us -> 37.3 us  [local(): pl.pallas_call(kernel, out_shape=pltpu.VMEM((tok, 8 * hd), BF16), in_spec...]
    unnamed x1, local copies, waits for them, and re-layouts: 2.26 us -> 0.97 us
where the time goes in v3:
time: 38.5 us; the launch traced here: 38.3 us
  Pallas kernels  37.3 us (97%)
  local copies, waits for them, and re-layouts  0.97 us (3%)
    pallas_call x1, Pallas kernels, local(): pl.pallas_call(kernel, out_shape=pltpu.VMEM((tok, 8 * hd), BF16), in_spec...  37.3 us
    unnamed x1, local copies, waits for them, and re-layouts  0.97 us

profile of v3, /device:TPU:448, one launch (start us, length us, event | category | flops | bytes accessed | tf_op | source)
XLA Modules:
  0.0 38.3 jit_solution(8487316480497175057)
XLA Ops:
  0.0 37.3 %shard_map.55 = bf16[512,1024]{1,0:T(8,128)(2,1)S(1)} custom-call(bf16[512,1024]{1,0:T(8,128)(2,1)} %q_hbm.1, bf16[512,1024]{1,0:T(8,128)(2,1)} %k_hbm.1, bf16[512,1024]{1,0:T(8,128)(2,1)} %v_hbm.1, f32[9,8,512]{2,1,0:T(8,128)} %w_hbm.1, f32[1,1024]{1,0:T(1,128)} %bitcast.1), custom_call_target="tpu_custom_call" | custom-call | flops 2000000000 | bytes 4400000 | tf_op jit(solution)/shard_map/pallas_call | solution.py:418
  37.4 1.0 %copy.7 = bf16[512,1024]{1,0:T(8,128)(2,1)} copy(bf16[512,1024]{1,0:T(8,128)(2,1)S(1)} %shard_map.55) | data formatting | bytes 2097152

commit v4 on v3

--- a/solution.py
+++ b/solution.py
@@ -19,7 +19,10 @@
 FAR_FIRST = (4, 3, 5, 2, 6, 1, 7)
 NEAR_FIRST = (1, 7, 2, 6, 3, 5, 4)
 PAIRS = ((0, 1), (0, 2), (1, 2), (2, 3), (0, 4), (1, 4), (2, 4), (3, 4), (4, 5), (4, 6), (5, 6), (6, 7))
-TARGETS = {a: [b for c, b in PAIRS if c == a] for a in range(RING - 1)}
+TO_FIRST = (1, 2, 3)
+FORWARD = PAIRS + ((0, 7),)
+GREET = FORWARD + ((0, 3),)
+TARGETS = {a: [b for c, b in FORWARD if c == a] for a in range(RING - 1)}
 MESH = pl.DeviceIdType.MESH
 F32 = jnp.float32
 BF16 = jnp.bfloat16
@@ -104,7 +107,7 @@
 
     for d in FAR_FIRST:
         greet(device(z, row_peer(d), core))
-    for a, b in PAIRS:
+    for a, b in GREET:
         pl.when(z == a)(lambda: greet(device(b, y, core)))
     greet(sibling)
     for d in range(1, COLS):
@@ -116,7 +119,7 @@
     g_load.start()
     for level in range(3):
 
-        @pl.when(jnp.logical_not(z_bits[level]))
+        @pl.when(jnp.logical_and(jnp.logical_not(z_bits[level]), z > 0))
         def _():
             high[:, mine, level * 128 : (level + 1) * 128] = jnp.zeros((HEADS_HERE, HALF, HEAD_DIM), BF16)
 
@@ -139,12 +142,12 @@
         own_bf[h] = s.astype(BF16)
         if i == 0:
             for row in range(RING):
-                rows_in = [a for a, b in PAIRS if b == row]
+                greeted = [a for a, b in GREET if b == row]
 
                 @pl.when(z == row)
                 def _():
-                    pl.semaphore_wait(barrier, 1 + RING - 1 + COLS - 1 + len(rows_in))
-                    for a in rows_in:
+                    pl.semaphore_wait(barrier, 1 + RING - 1 + COLS - 1 + len(greeted))
+                    for a in [a for a, b in FORWARD if b == row]:
                         pl.semaphore_signal(
                             ready.at[TARGETS[a].index(row)], inc=1, device_id=device(a, y, core), device_id_type=MESH
                         )
@@ -214,19 +217,21 @@
     s45 = part[4] + part[5]
     totals[z] = s0123 + (s45 + (part[6] + part[7]))
 
-    for a, b in PAIRS:
+    def to_row(a, b):
+        sem = tot_send.at[TARGETS[a].index(b) if a < b else 3]
+        first_in = min([c for c, t in PAIRS if t == b] or [0])
+        return remote(totals.at[a], totals.at[a], sem, tot_recv.at[a - first_in], device(b, y, core))
+
+    for a in TO_FIRST:
+        launch(to_row(a, 0), z == a)
+    for a, b in FORWARD:
 
         @pl.when(z == a)
         def _():
             pl.semaphore_wait(ready.at[TARGETS[a].index(b)], 1)
 
-        launch(
-            remote(
-                totals.at[a], totals.at[a], tot_send.at[TARGETS[a].index(b)],
-                tot_recv.at[a - b + (b & -b)], device(b, y, core),
-            ),
-            z == a,
-        )
+        if (a, b) in PAIRS:
+            launch(to_row(a, b), z == a)
 
     ring_sum[0] = s01.astype(BF16)
     ring_sum[1] = s45.astype(BF16)
@@ -241,6 +246,8 @@
 
     for d in FAR_FIRST:
         launch(low_copy(1, d), lax.rem(row_peer(d) // 2, 2) == 1, alone=False)
+    for d in FAR_FIRST:
+        launch(low_copy(2, d), jnp.logical_and(z == 0, row_peer(d) // 4 == 1), alone=False)
     for level in (1, 2):
         ends.append((y_bits[level], row_total(3, low_send.at[level - 1], ring_recv)))
         ends.append((jnp.logical_not(y_bits[level]), row_total(4, low_send.at[level - 1], ring_recv)))
@@ -257,18 +264,16 @@
         within(h)
 
     level_lanes = [slice(level * 128, (level + 1) * 128) for level in range(3)]
-    for row in range(1, RING):
-        rows_in = [a for a, b in PAIRS if b == row]
-        level = len(rows_in).bit_length() - 1
+    for row in range(RING):
+        rows_in = [a for a, b in PAIRS if b == row] if row else list(TO_FIRST)
+        level = len(rows_in).bit_length() - 1 if row else 2
 
         @pl.when(z == row)
         def _():
             for a in rows_in:
-                remote(
-                    totals.at[a], totals.at[a], tot_send.at[0], tot_recv.at[a - rows_in[0]], device(a, y, core)
-                ).wait_recv()
+                to_row(a, row).wait_recv()
             state = totals[rows_in[0]]
-            for a in rows_in[1:]:
+            for a in rows_in[1:] + [0] * (row == 0):
                 state = state + totals[a]
             high[y, mine, level_lanes[level]] = state.astype(BF16)
 
@@ -282,7 +287,7 @@
         )
 
     for d in FAR_FIRST:
-        launch(along_row(d), z > 0, alone=False)
+        launch(along_row(d), alone=False)
 
     @pl.when(core == 1)
     def _():
@@ -290,75 +295,90 @@
         for h in range(HEADS_HERE):
             acc[h] += w_cols[h, :, 2:3] * nn(q_s[h], core0[h])
 
-    when(z > 0, row_total(RING - 1, high_send, ring_recv).wait_send)
+    row_total(RING - 1, high_send, ring_recv).wait_send()
     for d in FAR_FIRST:
-        launch(low_copy(2, d), row_peer(d) // 4 == 1, alone=False)
+        launch(low_copy(2, d), jnp.logical_and(z > 0, row_peer(d) // 4 == 1), alone=False)
 
     def share_low(level):
         return remote(
             low.at[level, :, mine, :], low.at[level, :, mine, :], fwl_send.at[level], fwl_recv.at[level], sibling
         )
 
-    def low_arrivals():
-        for level in range(3):
-
-            @pl.when(y_bits[level])
-            def _():
-                if level == 0:
-                    to_next.wait_recv()
-                else:
-                    row_total(RING - 1, ring_send, low_recv.at[level - 1]).wait_recv()
-                share_low(level).start()
-
-        for level in range(3):
-
-            @pl.when(y_bits[level])
-            def _():
-                share_low(level).wait_recv()
-                for h in range(HEADS_HERE):
-                    acc[h] += w_cols[h, :, 3 + level : 4 + level] * nn(q_s[h], low[level, h])
-
-    for level in range(3):
-        ends.append((y_bits[level], share_low(level)))
-
-    pl.when(z == RING - 1)(low_arrivals)
+    arrivals = (0,) + NEAR_FIRST
 
     def share_high(i, h):
         return remote(high.at[h, mine, :], high.at[h, mine, :], fwh_send, fwh_recv.at[i], sibling)
 
-    def upward(level, i, h):
+    hop_to = jnp.where(z == 0, RING - 1, jnp.where(z == RING - 1, RING - 2, z + 1))
+
+    def hop(level, i, h):
         ref = high.at[h, mine, level_lanes[level]]
-        return remote(ref, ref, up_send.at[level - 1], up_recv.at[level - 1, i], device(lax.rem(z + 1, RING), y, core))
-
-    arrivals = (0,) + NEAR_FIRST
-    from_below = {1: lax.rem(z, 4) == 3, 2: z > 4}
-    go_up = {1: lax.rem(z, 4) == 2, 2: jnp.logical_and(z >= 4, z < 7)}
+        return remote(ref, ref, up_send.at[level - 1], up_recv.at[level - 1, i], device(hop_to, y, core))
+
+    odd = z_bits[0]
+    last = z == RING - 1
+    hops = {1: lax.rem(z, 4) == 2, 2: jnp.logical_or(lax.rem(z, 4) == 0, last)}
+    hop_in = {1: lax.rem(z, 4) == 3, 2: jnp.logical_or(z == 5, z == 6)}
     for i, d in enumerate(arrivals):
         h = lax.rem(y + RING - d, RING)
+        if d:
+            pl.when(jnp.logical_not(odd))(along_row(d).wait_recv)
+        pl.when(last)(hop(2, i, h).wait_recv)
         for level in (2, 1):
-            pl.when(from_below[level])(upward(level, i, h).wait_recv)
-        if d:
-            pl.when(z > 0)(along_row(d).wait_recv)
-        for level in (2, 1):
-            launch(upward(level, i, h), go_up[level], alone=False)
-        launch(share_high(i, h), alone=False)
-
-    whole = high.at[:, mine, :]
-    ends.append((None, remote(whole, whole, fwh_send, fwh_recv.at[0], sibling)))
+            launch(hop(level, i, h), hops[level], alone=False)
     for level in (1, 2):
-        ends.append((go_up[level], row_total(RING, up_send.at[level - 1], ring_recv)))
-    pl.when(z < RING - 1)(low_arrivals)
-
-    sq[...] = jnp.zeros_like(sq)
+        ends.append((hops[level], row_total(RING, up_send.at[level - 1], ring_recv)))
+
+    for level in range(3):
+
+        @pl.when(y_bits[level])
+        def _():
+            if level == 0:
+                to_next.wait_recv()
+            else:
+                row_total(RING - 1, ring_send, low_recv.at[level - 1]).wait_recv()
+
+        launch(share_low(level), y_bits[level])
+
     for i, d in enumerate(arrivals):
         h = lax.rem(y + RING - d, RING)
-        share_high(i, h).wait_recv()
-        r = nn(q_s[h], high[h])
-        a = acc[h]
-        for level in range(3):
-            a += w_cols[h, :, 6 + level : 7 + level] * r[:, level_lanes[level]]
-        acc[h] = a
-        sq[...] += a * a
+        if d:
+            pl.when(odd)(along_row(d).wait_recv)
+        for level in (1, 2):
+            pl.when(hop_in[level])(hop(level, i, h).wait_recv)
+        launch(share_high(i, h), z > 0, alone=False)
+    whole = high.at[:, mine, :]
+    ends.append((z > 0, remote(whole, whole, fwh_send, fwh_recv.at[0], sibling)))
+
+    for level in range(3):
+
+        @pl.when(y_bits[level])
+        def _():
+            share_low(level).wait_recv()
+            for h in range(HEADS_HERE):
+                acc[h] += w_cols[h, :, 3 + level : 4 + level] * nn(q_s[h], low[level, h])
+
+    @pl.when(z == 0)
+    def _():
+        total_sq = acc[0] * acc[0]
+        for h in range(1, HEADS_HERE):
+            total_sq += acc[h] * acc[h]
+        sq[...] = total_sq
+
+    @pl.when(z > 0)
+    def _():
+        for i, d in enumerate(arrivals):
+            h = lax.rem(y + RING - d, RING)
+            share_high(i, h).wait_recv()
+            r = nn(q_s[h], high[h])
+            a = acc[h]
+            for level in range(3):
+                a += w_cols[h, :, 6 + level : 7 + level] * r[:, level_lanes[level]]
+            acc[h] = a
+            if i == 0:
+                sq[...] = a * a
+            else:
+                sq[...] += a * a
 
     sq_in[col, 0:1, :] = jnp.sum(sq[...].T, axis=0, keepdims=True)
 
@@ -410,9 +430,9 @@
         pltpu.VMEM((8, tok, hd), F32),
         pltpu.VMEM((tok, hd), F32),
         pltpu.VMEM((COLS, 8, tok), F32),
-        dma((8,)), dma((3,)), pltpu.SemaphoreType.REGULAR((3,)),
+        dma((8,)), dma((3,)), pltpu.SemaphoreType.REGULAR((4,)),
         dma, dma((8,)), dma, dma, dma, dma, dma, dma,
-        dma((2,)), dma((2,)), dma((3,)), dma((4,)), dma, dma((7,)), dma((2,)), dma((2, 8)),
+        dma((2,)), dma((2,)), dma((4,)), dma((4,)), dma, dma((7,)), dma((2,)), dma((2, 8)),
         dma((3,)), dma((3,)), dma, dma((8,)), dma, dma,
     ]
     return pl.pallas_call(

time: 38.5 us -> 35.5 us (0.922)
  the two profiles are of different devices: /device:TPU:448 before, /device:TPU:384 now
where the time goes in v4:
time: 35.5 us; the launch traced here: 35.4 us
  Pallas kernels  34.4 us (97%)
  local copies, waits for them, and re-layouts  0.97 us (3%)
    pallas_call x1, Pallas kernels, local(): pl.pallas_call(kernel, out_shape=pltpu.VMEM((tok, 8 * hd), BF16), in_spec...  34.4 us
    unnamed x1, local copies, waits for them, and re-layouts  0.97 us

profile of v4, /device:TPU:384, one launch (start us, length us, event | category | flops | bytes accessed | tf_op | source)
XLA Modules:
  0.0 35.4 jit_solution(13455483506917905555)
XLA Ops:
  0.0 34.4 %shard_map.55 = bf16[512,1024]{1,0:T(8,128)(2,1)S(1)} custom-call(bf16[512,1024]{1,0:T(8,128)(2,1)} %q_hbm.1, bf16[512,1024]{1,0:T(8,128)(2,1)} %k_hbm.1, bf16[512,1024]{1,0:T(8,128)(2,1)} %v_hbm.1, f32[9,8,512]{2,1,0:T(8,128)} %w_hbm.1, f32[1,1024]{1,0:T(1,128)} %bitcast.1), custom_call_target="tpu_custom_call" | custom-call | flops 2000000000 | bytes 4400000 | tf_op jit(solution)/shard_map/pallas_call | solution.py:438
  34.4 1.0 %copy.7 = bf16[512,1024]{1,0:T(8,128)(2,1)} copy(bf16[512,1024]{1,0:T(8,128)(2,1)S(1)} %shard_map.55) | data formatting | bytes 2097152

commit v5 on v4

--- a/solution.py
+++ b/solution.py
@@ -14,13 +14,14 @@
 COLS = 4
 HEADS_HERE = 8
 TOK = 512
+LAG = 3
 EARLY = 5
 HALF = 64
 FAR_FIRST = (4, 3, 5, 2, 6, 1, 7)
 NEAR_FIRST = (1, 7, 2, 6, 3, 5, 4)
 PAIRS = ((0, 1), (0, 2), (1, 2), (2, 3), (0, 4), (1, 4), (2, 4), (3, 4), (4, 5), (4, 6), (5, 6), (6, 7))
 TO_FIRST = (1, 2, 3)
-FORWARD = PAIRS + ((0, 7),)
+FORWARD = PAIRS + ((0, 6), (0, 7))
 GREET = FORWARD + ((0, 3),)
 TARGETS = {a: [b for c, b in FORWARD if c == a] for a in range(RING - 1)}
 MESH = pl.DeviceIdType.MESH
@@ -122,6 +123,10 @@
         @pl.when(jnp.logical_and(jnp.logical_not(z_bits[level]), z > 0))
         def _():
             high[:, mine, level * 128 : (level + 1) * 128] = jnp.zeros((HEADS_HERE, HALF, HEAD_DIM), BF16)
+
+    @pl.when(jnp.logical_not(y_bits[2]))
+    def _():
+        high[:, :, 384:512] = jnp.zeros((HEADS_HERE, HEAD_DIM, HEAD_DIM), BF16)
 
     to_sibling = []
     for i, d in enumerate(order):
@@ -240,8 +245,9 @@
     def low_copy(level, d):
         target = row_peer(d)
         src = ring_sum.at[target // 4] if level == 1 else ring_sum.at[2]
+        dst = low.at[1, y, mine, :] if level == 1 else high.at[y, mine, 384:512]
         return remote(
-            src, low.at[level, y, mine, :], low_send.at[level - 1], low_recv.at[level - 1], device(z, target, core)
+            src, dst, low_send.at[level - 1], low_recv.at[level - 1], device(z, target, core)
         )
 
     for d in FAR_FIRST:
@@ -258,7 +264,7 @@
 
     @pl.when(y_bits[2])
     def _():
-        low[2, y, mine, :] = ring_sum[2]
+        high[y, mine, 384:512] = ring_sum[2]
 
     for h in range(EARLY, HEADS_HERE):
         within(h)
@@ -286,7 +292,7 @@
             device(z, row_peer(d), core),
         )
 
-    for d in FAR_FIRST:
+    for d in NEAR_FIRST:
         launch(along_row(d), alone=False)
 
     @pl.when(core == 1)
@@ -300,85 +306,97 @@
         launch(low_copy(2, d), jnp.logical_and(z > 0, row_peer(d) // 4 == 1), alone=False)
 
     def share_low(level):
-        return remote(
-            low.at[level, :, mine, :], low.at[level, :, mine, :], fwl_send.at[level], fwl_recv.at[level], sibling
-        )
-
-    arrivals = (0,) + NEAR_FIRST
-
-    def share_high(i, h):
-        return remote(high.at[h, mine, :], high.at[h, mine, :], fwh_send, fwh_recv.at[i], sibling)
-
-    hop_to = jnp.where(z == 0, RING - 1, jnp.where(z == RING - 1, RING - 2, z + 1))
-
-    def hop(level, i, h):
-        ref = high.at[h, mine, level_lanes[level]]
-        return remote(ref, ref, up_send.at[level - 1], up_recv.at[level - 1, i], device(hop_to, y, core))
-
-    odd = z_bits[0]
-    last = z == RING - 1
-    hops = {1: lax.rem(z, 4) == 2, 2: jnp.logical_or(lax.rem(z, 4) == 0, last)}
-    hop_in = {1: lax.rem(z, 4) == 3, 2: jnp.logical_or(z == 5, z == 6)}
-    for i, d in enumerate(arrivals):
-        h = lax.rem(y + RING - d, RING)
-        if d:
-            pl.when(jnp.logical_not(odd))(along_row(d).wait_recv)
-        pl.when(last)(hop(2, i, h).wait_recv)
-        for level in (2, 1):
-            launch(hop(level, i, h), hops[level], alone=False)
-    for level in (1, 2):
-        ends.append((hops[level], row_total(RING, up_send.at[level - 1], ring_recv)))
-
-    for level in range(3):
-
-        @pl.when(y_bits[level])
+        part = low.at[level, :, mine, :] if level < 2 else high.at[:, mine, 384:512]
+        return remote(part, part, fwl_send.at[level], fwl_recv.at[level], sibling)
+
+    def low_arrival(level, cond):
+        @pl.when(cond)
         def _():
             if level == 0:
                 to_next.wait_recv()
             else:
                 row_total(RING - 1, ring_send, low_recv.at[level - 1]).wait_recv()
-
-        launch(share_low(level), y_bits[level])
-
-    for i, d in enumerate(arrivals):
-        h = lax.rem(y + RING - d, RING)
-        if d:
-            pl.when(odd)(along_row(d).wait_recv)
-        for level in (1, 2):
-            pl.when(hop_in[level])(hop(level, i, h).wait_recv)
-        launch(share_high(i, h), z > 0, alone=False)
-    whole = high.at[:, mine, :]
-    ends.append((z > 0, remote(whole, whole, fwh_send, fwh_recv.at[0], sibling)))
+            share_low(level).start()
 
     for level in range(3):
-
+        ends.append((y_bits[level], share_low(level)))
+    low_arrival(0, y_bits[0])
+    low_arrival(1, y_bits[1])
+    low_arrival(2, jnp.logical_and(y_bits[2], z == 0))
+
+    def low_readout(level):
         @pl.when(y_bits[level])
         def _():
             share_low(level).wait_recv()
             for h in range(HEADS_HERE):
                 acc[h] += w_cols[h, :, 3 + level : 4 + level] * nn(q_s[h], low[level, h])
 
+    arrivals = (0,) + NEAR_FIRST
+
+    def share_high(i, h):
+        part = high.at[h, mine, 0:384]
+        return remote(part, part, fwh_send, fwh_recv.at[i], sibling)
+
+    def hop(level, i, h, to):
+        ref = high.at[h, mine, level_lanes[level]]
+        return remote(ref, ref, up_send.at[level - 1], up_recv.at[level - 1, i], device(to, y, core))
+
+    odd = z_bits[0]
+    above = lax.rem(z + 1, RING)
+    hop_in = {1: lax.rem(z, 4) == 3, 2: z > 4}
     @pl.when(z == 0)
     def _():
-        total_sq = acc[0] * acc[0]
-        for h in range(1, HEADS_HERE):
-            total_sq += acc[h] * acc[h]
-        sq[...] = total_sq
+        low_readout(0)
+        low_readout(1)
+        pl.when(y_bits[2])(share_low(2).wait_recv)
+        for h in range(HEADS_HERE):
+            a = acc[h] + w_cols[h, :, 5:6] * nn(q_s[h], high[h, :, 384:512])
+            acc[h] = a
+            sq[...] = a * a if h == 0 else sq[...] + a * a
+
+    for i, d in enumerate(arrivals):
+        h = lax.rem(y + RING - d, RING)
+        if d:
+            pl.when(jnp.logical_not(odd))(along_row(d).wait_recv)
+        for to in (RING - 2, RING - 1):
+            launch(hop(2, i, h, to), z == 0, alone=False)
+        launch(hop(2, i, h, above), z == 4, alone=False)
+        launch(hop(1, i, h, above), lax.rem(z, 4) == 2, alone=False)
+    ends.append((lax.rem(z, 4) == 2, row_total(RING, up_send.at[0], ring_recv)))
+    ends.append((z == 4, row_total(RING, up_send.at[1], ring_recv)))
+    ends.append((z == 0, remote(low.at[0], low.at[0], up_send.at[1], ring_recv, sibling)))
+
+    def readout(i, d):
+        h = lax.rem(y + RING - d, RING)
+        share_high(i, h).wait_recv()
+        r = nn(q_s[h], high[h])
+        a = acc[h] + w_cols[h, :, 5:6] * r[:, 384:512]
+        for level in range(3):
+            a += w_cols[h, :, 6 + level : 7 + level] * r[:, level_lanes[level]]
+        acc[h] = a
+        sq[...] = a * a if i == 0 else sq[...] + a * a
 
     @pl.when(z > 0)
     def _():
+        low_readout(0)
+        low_readout(1)
+        low_arrival(2, y_bits[2])
         for i, d in enumerate(arrivals):
             h = lax.rem(y + RING - d, RING)
-            share_high(i, h).wait_recv()
-            r = nn(q_s[h], high[h])
-            a = acc[h]
-            for level in range(3):
-                a += w_cols[h, :, 6 + level : 7 + level] * r[:, level_lanes[level]]
-            acc[h] = a
-            if i == 0:
-                sq[...] = a * a
-            else:
-                sq[...] += a * a
+            if d:
+                pl.when(odd)(along_row(d).wait_recv)
+            for level in (1, 2):
+                pl.when(hop_in[level])(hop(level, i, h, above).wait_recv)
+            share_high(i, h).start()
+            if i == LAG:
+                pl.when(y_bits[2])(share_low(2).wait_recv)
+            if i >= LAG:
+                readout(i - LAG, arrivals[i - LAG])
+        for i in range(RING - LAG, RING):
+            readout(i, arrivals[i])
+
+    whole = high.at[:, mine, 0:384]
+    ends.append((z > 0, remote(whole, whole, fwh_send, fwh_recv.at[0], sibling)))
 
     sq_in[col, 0:1, :] = jnp.sum(sq[...].T, axis=0, keepdims=True)
 
@@ -425,12 +443,12 @@
         pltpu.VMEM((ring, half, hd), BF16),
         pltpu.VMEM((3, half, hd), BF16),
         pltpu.VMEM((ring, half, hd), F32),
-        pltpu.VMEM((3, 8, hd, hd), BF16),
-        pltpu.VMEM((8, hd, 3 * hd), BF16),
+        pltpu.VMEM((2, 8, hd, hd), BF16),
+        pltpu.VMEM((8, hd, 4 * hd), BF16),
         pltpu.VMEM((8, tok, hd), F32),
         pltpu.VMEM((tok, hd), F32),
         pltpu.VMEM((COLS, 8, tok), F32),
-        dma((8,)), dma((3,)), pltpu.SemaphoreType.REGULAR((4,)),
+        dma((8,)), dma((3,)), pltpu.SemaphoreType.REGULAR((5,)),
         dma, dma((8,)), dma, dma, dma, dma, dma, dma,
         dma((2,)), dma((2,)), dma((4,)), dma((4,)), dma, dma((7,)), dma((2,)), dma((2, 8)),
         dma((3,)), dma((3,)), dma, dma((8,)), dma, dma,

time: 35.5 us -> 34 us (0.958)
  the two profiles are of different devices: /device:TPU:384 before, /device:TPU:448 now
where the time goes in v5:
time: 34 us; the launch traced here: 33.9 us
  Pallas kernels  32.9 us (97%)
  local copies, waits for them, and re-layouts  0.97 us (3%)
    pallas_call x1, Pallas kernels, local(): pl.pallas_call(kernel, out_shape=pltpu.VMEM((tok, 8 * hd), BF16), in_spec...  32.9 us
    unnamed x1, local copies, waits for them, and re-layouts  0.97 us

profile of v5, /device:TPU:448, one launch (start us, length us, event | category | flops | bytes accessed | tf_op | source)
XLA Modules:
  0.0 33.9 jit_solution(5094873819574126690)
XLA Ops:
  0.0 32.9 %shard_map.55 = bf16[512,1024]{1,0:T(8,128)(2,1)S(1)} custom-call(bf16[512,1024]{1,0:T(8,128)(2,1)} %q_hbm.1, bf16[512,1024]{1,0:T(8,128)(2,1)} %k_hbm.1, bf16[512,1024]{1,0:T(8,128)(2,1)} %v_hbm.1, f32[9,8,512]{2,1,0:T(8,128)} %w_hbm.1, f32[1,1024]{1,0:T(1,128)} %bitcast.1), custom_call_target="tpu_custom_call" | custom-call | flops 2000000000 | bytes 4400000 | tf_op jit(solution)/shard_map/pallas_call | solution.py:456
  32.9 1.0 %copy.7 = bf16[512,1024]{1,0:T(8,128)(2,1)} copy(bf16[512,1024]{1,0:T(8,128)(2,1)S(1)} %shard_map.55) | data formatting | bytes 2097152

commit v6 on v5

--- a/solution.py
+++ b/solution.py
@@ -15,7 +15,7 @@
 HEADS_HERE = 8
 TOK = 512
 LAG = 3
-EARLY = 5
+EARLY = 3
 HALF = 64
 FAR_FIRST = (4, 3, 5, 2, 6, 1, 7)
 NEAR_FIRST = (1, 7, 2, 6, 3, 5, 4)
@@ -409,6 +409,8 @@
     for d in (2, 1, 3):
         launch(to_cols(d), alone=False)
     g_load.wait()
+    for h in range(HEADS_HERE):
+        acc[h] = acc[h] * g_v[:, h * HEAD_DIM : (h + 1) * HEAD_DIM]
     others = sq_in.at[0 : COLS - 1, 0:1]
     from_cols = remote(others, others, sq_send, sq_recv, (seq, lax.rem(col + 1, COLS)))
     ends.append((None, from_cols))
@@ -419,7 +421,7 @@
 
     for h in range(HEADS_HERE):
         columns = slice(h * HEAD_DIM, (h + 1) * HEAD_DIM)
-        out[:, columns] = (acc[h] * scale * g_v[:, columns]).astype(BF16)
+        out[:, columns] = (acc[h] * scale).astype(BF16)
     finish()
 
 

time: 34 us -> 33.7 us (level)
  Pallas kernels: 32.9 us -> 32.5 us
    pallas_call x1, Pallas kernels: 32.9 us -> 32.5 us  [local(): pl.pallas_call(kernel, out_shape=pltpu.VMEM((tok, 8 * hd), BF16), in_spec...]
where the time goes in v6:
time: 33.7 us; the launch traced here: 33.5 us
  Pallas kernels  32.5 us (96%)
  local copies, waits for them, and re-layouts  0.97 us (3%)
    pallas_call x1, Pallas kernels, local(): pl.pallas_call(kernel, out_shape=pltpu.VMEM((tok, 8 * hd), BF16), in_spec...  32.5 us
    unnamed x1, local copies, waits for them, and re-layouts  0.97 us

profile of v6, /device:TPU:448, one launch (start us, length us, event | category | flops | bytes accessed | tf_op | source)
XLA Modules:
  0.0 33.5 jit_solution(13772571985940498338)
XLA Ops:
  0.0 32.5 %shard_map.55 = bf16[512,1024]{1,0:T(8,128)(2,1)S(1)} custom-call(bf16[512,1024]{1,0:T(8,128)(2,1)} %q_hbm.1, bf16[512,1024]{1,0:T(8,128)(2,1)} %k_hbm.1, bf16[512,1024]{1,0:T(8,128)(2,1)} %v_hbm.1, f32[9,8,512]{2,1,0:T(8,128)} %w_hbm.1, f32[1,1024]{1,0:T(1,128)} %bitcast.1), custom_call_target="tpu_custom_call" | custom-call | flops 2000000000 | bytes 4400000 | tf_op jit(solution)/shard_map/pallas_call | solution.py:458
  32.5 1.0 %copy.7 = bf16[512,1024]{1,0:T(8,128)(2,1)} copy(bf16[512,1024]{1,0:T(8,128)(2,1)S(1)} %shard_map.55) | data formatting | bytes 2097152

commit v7 on v6

--- a/solution.py
+++ b/solution.py
@@ -95,9 +95,13 @@
     def columns_of(i):
         return pl.ds(pl.multiple_of(row_peer(order[i]) * HEAD_DIM, HEAD_DIM), HEAD_DIM)
 
-    for i, d in enumerate(order):
-        pltpu.make_async_copy(k_hbm.at[:, columns_of(i)], kv_s.at[row_peer(d), 0], load_sem.at[i]).start()
-        pltpu.make_async_copy(v_hbm.at[:, columns_of(i)], kv_s.at[row_peer(d), 1], load_sem.at[i]).start()
+    def load_kv(i):
+        h = row_peer(order[i])
+        pltpu.make_async_copy(k_hbm.at[:, columns_of(i)], kv_s.at[h, 0], load_sem.at[i]).start()
+        pltpu.make_async_copy(v_hbm.at[:, columns_of(i)], kv_s.at[h, 1], load_sem.at[i]).start()
+
+    for i in range(2):
+        load_kv(i)
     w_load = pltpu.make_async_copy(w_hbm, w_v, misc_sem.at[0])
     g_load = pltpu.make_async_copy(g_hbm, g_v, misc_sem.at[1])
 
@@ -108,6 +112,8 @@
 
     for d in FAR_FIRST:
         greet(device(z, row_peer(d), core))
+    for i in range(2, HEADS_HERE):
+        load_kv(i)
     for a, b in GREET:
         pl.when(z == a)(lambda: greet(device(b, y, core)))
     greet(sibling)

time: 33.7 us -> 33.6 us (level)
  no operation moved by 1% of the time
where the time goes in v7:
time: 33.6 us; the launch traced here: 33.2 us
  Pallas kernels  32.2 us (96%)
  local copies, waits for them, and re-layouts  0.97 us (3%)
    pallas_call x1, Pallas kernels, local(): pl.pallas_call(kernel, out_shape=pltpu.VMEM((tok, 8 * hd), BF16), in_spec...  32.2 us
    unnamed x1, local copies, waits for them, and re-layouts  0.97 us

profile of v7, /device:TPU:448, one launch (start us, length us, event | category | flops | bytes accessed | tf_op | source)
XLA Modules:
  0.0 33.2 jit_solution(13544344423769769854)
XLA Ops:
  0.0 32.2 %shard_map.55 = bf16[512,1024]{1,0:T(8,128)(2,1)S(1)} custom-call(bf16[512,1024]{1,0:T(8,128)(2,1)} %q_hbm.1, bf16[512,1024]{1,0:T(8,128)(2,1)} %k_hbm.1, bf16[512,1024]{1,0:T(8,128)(2,1)} %v_hbm.1, f32[9,8,512]{2,1,0:T(8,128)} %w_hbm.1, f32[1,1024]{1,0:T(1,128)} %bitcast.1), custom_call_target="tpu_custom_call" | custom-call | flops 2000000000 | bytes 4400000 | tf_op jit(solution)/shard_map/pallas_call | solution.py:464
  32.2 1.0 %copy.7 = bf16[512,1024]{1,0:T(8,128)(2,1)} copy(bf16[512,1024]{1,0:T(8,128)(2,1)S(1)} %shard_map.55) | data formatting | bytes 2097152
